TPU v7x, 32 devices: a whole 2x2x4 slice. The times are simulated.
32 devices in a mesh: gx: 4 (over z), gy: 2 (over x), gz: 4 (over y, core).
Axes of the slice: x: 2, y: 2, z: 4, core: 2. Of those that a mesh axis runs over, the one named last changes fastest.
Arguments:
- dual_blocks: bfloat16 [4, 2, 4, 1024, 1024], P('gx', 'gy', 'gz'), may hold values from -1 to 3, as said below
- load_terms: bfloat16 [4, 2, 4, 1024, 128], P('gx', 'gy', 'gz'), may hold values from -6 to 6
- row_order: int32 [4, 2, 4, 1024], P('gx', 'gy', 'gz'), may hold values from 0 to 1023, each once within a row
- mode_rows: bfloat16 [4, 2, 4, 1024, 6], P('gx', 'gy', 'gz'), may hold values from -0.1875 to 0.1875
- mode_count: int32 [4, 2, 4], P('gx', 'gy', 'gz'), may hold values from 0 to 6, as said below
- coarse_inverse: float32 [4, 2, 24, 24], P('gx', 'gy'), may hold values from -1 to 3, as said below
Outputs:
- multipliers: float32 [4, 2, 4, 1024, 128], P('gx', 'gy', 'gz')
- residual: float32 [4, 2, 4, 1024, 128], P('gx', 'gy', 'gz')
Inputs may be any that keep to these rules, and one draw needn't show every extreme that they name: `mode_count`: subdomains away from the outer boundary have 6 rigid-body modes; subdomains on the outer boundary have 0 to 6; some subdomain has exactly 6 and some boundary subdomain has none. Each subdomain's row of row_order is a permutation of its 1024 rows. `dual_blocks`: each subdomain's block is symmetric positive definite. `coarse_inverse`: each line's matrix is symmetric positive definite.
All inputs are finite; a program needn't handle non-finite values.
Results may differ from a plain program's by a relative error of at most 0.0082.
Values sent between devices are 32-bit elements; how exact they have to be, the bound alone decides.
A program may use at most 64 MiB of HBM per device.

v0:
```python
import jax
import jax.numpy as jnp
from jax import lax
from jax.sharding import PartitionSpec as P

FACE = 128
EDGE = 16
CORNER = 8
NMODE = 6
ITERS = 3


EIG_LOW = 0.5
EIG_HIGH = 6.0


def from_behind(block, axis, distance):
    devices = range(lax.axis_size(axis))
    route = [(i - distance, i) for i in devices if i - distance in devices]
    return lax.ppermute(block, axis, route)


def slot_table():
    slot_list = []
    begin_row = 0
    for weight_class, width_rows in ((1, FACE), (2, EDGE), (3, CORNER)):
        for sign_one in (-1, 0, 1):
            for sign_two in (-1, 0, 1):
                for sign_three in (-1, 0, 1):
                    if abs(sign_one) + abs(sign_two) + abs(sign_three) == weight_class:
                        slot_list.append(((sign_one, sign_two, sign_three), begin_row, width_rows))
                        begin_row += width_rows
    return slot_list


def partner(packed):
    slot_list = slot_table()
    travelling = []
    for offset, begin_row, width_rows in slot_list:
        travelling.append([offset, list(offset), packed[begin_row : begin_row + width_rows]])
    for axis_pos in range(3):
        for heading in (1, -1):
            chosen = [record for record in travelling if record[1][axis_pos] == heading]
            bundle = jnp.concatenate([record[2] for record in chosen], axis=0)
            if axis_pos == 0:
                arrived = from_behind(bundle, "gx", heading)
            elif axis_pos == 1:
                arrived = from_behind(bundle, "gy", heading)
            else:
                arrived = from_behind(bundle, "gz", heading)
            cursor = 0
            for record in chosen:
                row_count = record[2].shape[0]
                record[2] = arrived[cursor : cursor + row_count]
                record[1][axis_pos] = 0
                cursor += row_count
    by_anchor = {}
    for record in travelling:
        by_anchor[record[0]] = record[2]
    return jnp.concatenate(
        [
            by_anchor[-offset[0], -offset[1], -offset[2]]
            for offset, begin_row, width_rows in slot_list
        ],
        axis=0,
    )


def coarse_amplitude(residual, mode_cols, count_value, inverse):
    highest = lax.Precision.HIGHEST
    project = jnp.dot(mode_cols.T, residual, precision=highest, preferred_element_type=jnp.float32)
    everyone, counts = (
        lax.all_gather(project, "gz", axis=0, tiled=True),
        lax.all_gather(count_value, "gz", axis=0, tiled=True),
    )
    coarse_size = inverse.shape[0]
    line_length = lax.axis_size("gz")
    offsets = jnp.cumsum(counts) - counts
    owner_offset = jnp.repeat(offsets, NMODE)
    owner_count = jnp.repeat(counts, NMODE)
    within = jnp.tile(jnp.arange(NMODE, dtype=jnp.float32), line_length)
    compact_pos = jnp.arange(coarse_size, dtype=jnp.float32)[:, None]
    hits = compact_pos == (owner_offset + within)[None, :]
    valid = (within < owner_count)[None, :]
    select = jnp.where(hits & valid, 1.0, 0.0).astype(jnp.float32)
    compact = jnp.dot(select, everyone, precision=highest, preferred_element_type=jnp.float32)
    select_mine = lax.dynamic_slice_in_dim(select, lax.axis_index("gz") * NMODE, NMODE, 1)
    rows_mine = jnp.dot(
        select_mine.T, inverse, precision=highest, preferred_element_type=jnp.float32
    )
    return jnp.dot(rows_mine, compact, precision=highest, preferred_element_type=jnp.float32)


def precondition(residual, mode_cols, count_value, inverse):
    highest = lax.Precision.HIGHEST
    amplitude = coarse_amplitude(residual, mode_cols, count_value, inverse)
    spread = jnp.dot(mode_cols, amplitude, precision=highest, preferred_element_type=jnp.float32)
    remote_part = partner(spread)
    return residual - spread - remote_part


def apply_operator(dual_packed, direction):
    rounded = direction.astype(jnp.bfloat16)
    local_image = jnp.dot(dual_packed, rounded, preferred_element_type=jnp.float32)
    return local_image + partner(local_image)


def chebyshev(load_rows, dual_packed, mode_cols, count_value, inverse):
    center_value = 0.5 * (EIG_HIGH + EIG_LOW)
    half_width = 0.5 * (EIG_HIGH - EIG_LOW)
    residual = load_rows + partner(load_rows)
    direction = precondition(residual, mode_cols, count_value, inverse) / center_value
    multipliers = direction
    rho_prev = half_width / center_value
    residual = residual - apply_operator(dual_packed, direction)
    for iteration in range(1, ITERS):
        corrected = precondition(residual, mode_cols, count_value, inverse)
        rho_now = 1.0 / (2.0 * center_value / half_width - rho_prev)
        direction = rho_now * rho_prev * direction + 2.0 * rho_now / half_width * corrected
        multipliers = multipliers + direction
        residual = residual - apply_operator(dual_packed, direction)
        rho_prev = rho_now
    return (multipliers, residual)


def local(dual_blocks, load_terms, row_order, mode_rows, mode_count, coarse_inverse):
    packing = row_order[0, 0, 0]
    dual_packed = jnp.take(jnp.take(dual_blocks[0, 0, 0], packing, axis=0), packing, axis=1)
    load_rows = jnp.take(load_terms[0, 0, 0], packing, axis=0).astype(jnp.float32)
    mode_cols = jnp.take(mode_rows[0, 0, 0], packing, axis=0).astype(jnp.float32)
    count_value = mode_count.reshape(1).astype(jnp.float32)
    inverse = coarse_inverse[0, 0]
    multipliers, residual = chebyshev(load_rows, dual_packed, mode_cols, count_value, inverse)
    unpacking = jnp.argsort(packing)
    return (
        jnp.take(multipliers, unpacking, axis=0)[None, None, None],
        jnp.take(residual, unpacking, axis=0)[None, None, None],
    )


def solution(mesh):
    in_specs = (
        P("gx", "gy", "gz", None, None),
        P("gx", "gy", "gz", None, None),
        P("gx", "gy", "gz", None),
        P("gx", "gy", "gz", None, None),
        P("gx", "gy", "gz"),
        P("gx", "gy", None, None),
    )
    out_specs = (P("gx", "gy", "gz", None, None), P("gx", "gy", "gz", None, None))
    return jax.shard_map(local, mesh=mesh, in_specs=in_specs, out_specs=out_specs, check_vma=False)
```

profile of v0, /device:TPU:1, one launch (start us, length us, event | category | flops | bytes accessed | tf_op | source)
XLA Modules:
  0.0 301.7 jit_solution(11585759530583108009)
XLA Ops:
  2.2 5.1 %sort.17 = (s32[1024]{0:T(1024)}, s32[1024]{0:T(1024)S(1)}) sort(s32[1024]{0:T(1024)} %bitcast.44, s32[1024]{0:T(1024)S(1)} %iota.16), dimensions={0}, to_apply=%region_1.2 | sort | flops 10240 | bytes 16384 | tf_op jit(solution)/shard_map/jit(argsort)/sort | solution.py:134
  7.3 3.9 %gather_fusion = bf16[1024,128]{1,0:T(8,128)(2,1)S(1)} fusion(bf16[1024,128]{1,0:T(8,128)(2,1)} %bitcast.42, s32[1024]{0:T(1024)S(1)} %get-tuple-element.255), kind=kCustom, calls=%fused_computation.2 | custom fusion | bytes 528384 | tf_op jit(solution)/shard_map/jit(_take)/gather | solution.py:129
  16.2 6.4 %all-reduce = f32[4]{0:T(128)S(1)} all-reduce(f32[4]{0:T(128)S(1)} %bitcast_dynamic-update-slice_fusion), channel_id=2, replica_groups=mesh['gx'=4,'gy'=2,'gz'=4] {'gz'}, use_global_device_ids=true, to_apply=%add | all-reduce | flops 4 | bytes 32 | tf_op jit(solution)/shard_map/all_gather | solution.py:74
  23.3 3.2 %gather_fusion.1 = bf16[1024,6]{1,0:T(8,128)(2,1)S(1)} fusion(bf16[1024,6]{1,0:T(8,128)(2,1)S(1)} %bitcast.41, s32[1024]{0:T(1024)S(1)} %get-tuple-element.255), kind=kCustom, calls=%fused_computation.3 | custom fusion | bytes 28672 | tf_op jit(solution)/shard_map/jit(_take)/gather | solution.py:130
  28.5 4.3 %collective-permute-start = (f32[224,128]{1,0:T(8,128)S(1)}, f32[224,128]{1,0:T(8,128)S(1)}, u32[]{:S(2)}, u32[]{:S(2)}) collective-permute-start(f32[224,128]{1,0:T(8,128)S(1)} %pad_maximum_fusion), channel_id=1, source_target_pairs={{0,8},{8,16},{16,24},{1,9},{9,17},{17,25},{2,10},{10,18},{18,26},{... | collective-permute-start | bytes 344072 | tf_op jit(solution)/shard_map/ppermute | solution.py:20
  37.8 4.0 %collective-permute-start.2 = (f32[224,128]{1,0:T(8,128)}, f32[224,128]{1,0:T(8,128)S(1)}, u32[]{:S(2)}, u32[]{:S(2)}) collective-permute-start(f32[224,128]{1,0:T(8,128)} %get-tuple-element.247), channel_id=1, source_target_pairs={{0,4},{1,5},{2,6},{3,7},{8,12},{9,13},{10,14},{11,15},{16,20},{17,... | collective-permute-start | bytes 344072 | tf_op jit(solution)/shard_map/ppermute | solution.py:20
  47.4 5.3 %collective-permute-start.5 = (f32[224,128]{1,0:T(8,128)}, f32[224,128]{1,0:T(8,128)S(1)}, u32[]{:S(2)}, u32[]{:S(2)}) collective-permute-start(f32[224,128]{1,0:T(8,128)} %get-tuple-element.228), channel_id=1, source_target_pairs={{1,0},{2,1},{3,2},{5,4},{6,5},{7,6},{9,8},{10,9},{11,10},{13,12},{... | collective-permute-start | bytes 344072 | tf_op jit(solution)/shard_map/ppermute | solution.py:20
  58.3 5.8 %all-gather.1 = f32[4,6,128]{2,1,0:T(8,128)S(1)} all-gather(f32[1,6,128]{2,1,0:T(8,128)S(1)} %convolution_bitcast_fusion.2), channel_id=1, replica_groups=mesh['gx'=4,'gy'=2,'gz'=4] {'gz'}, dimensions={0}, use_global_device_ids=true | all-gather | bytes 15360 | tf_op jit(solution)/shard_map/all_gather | solution.py:73
  70.1 5.4 %gather_fusion.2 = bf16[1024,1024]{1,0:T(8,128)(2,1)} fusion(bf16[1024,1024]{1,0:T(8,128)(2,1)S(1)} %bitcast.40, s32[1024]{0:T(1024)S(1)} %get-tuple-element.255), kind=kCustom, calls=%fused_computation.4 | custom fusion | bytes 4198400 | tf_op jit(solution)/shard_map/jit(_take)/gather | solution.py:128
  78.3 3.9 %collective-permute-start.6 = (f32[224,128]{1,0:T(8,128)S(1)}, f32[224,128]{1,0:T(8,128)S(1)}, u32[]{:S(2)}, u32[]{:S(2)}) collective-permute-start(f32[224,128]{1,0:T(8,128)S(1)} %pad_maximum_fusion.2), channel_id=1, source_target_pairs={{0,8},{8,16},{16,24},{1,9},{9,17},{17,25},{2,10},{10,18},{18,26},{... | collective-permute-start | bytes 344072 | tf_op jit(solution)/shard_map/ppermute | solution.py:20
  82.3 3.2 %broadcast_select_fusion = bf16[1024,1024]{1,0:T(8,128)(2,1)} fusion(bf16[1024,1024]{1,0:T(8,128)(2,1)} %gather_fusion.2, pred[1024]{0:T(1024)(128)(4,1)S(1)} %compare_and_fusion.1), kind=kLoop, calls=%fused_computation.6 | loop fusion | flops 1048576 | bytes 4195328 | tf_op jit(solution)/shard_map/jit(_take)/select_n | solution.py:128
  85.4 3.9 %copy.13 = bf16[1024,1024]{0,1:T(8,128)(2,1)} copy(bf16[1024,1024]{1,0:T(8,128)(2,1)} %broadcast_select_fusion) | data formatting | bytes 4194304 | tf_op jit(solution)/shard_map/jit(_take)/select_n | solution.py:128
  89.4 7.9 %gather_fusion.3 = bf16[1024,1024]{1,0:T(8,128)(2,1)} fusion(bf16[1024,1024]{0,1:T(8,128)(2,1)} %copy.13, s32[1024]{0:T(1024)S(1)} %get-tuple-element.255), kind=kCustom, calls=%fused_computation.5 | custom fusion | bytes 4198400 | tf_op jit(solution)/shard_map/jit(_take)/gather | solution.py:128
  101.2 4.0 %collective-permute-start.8 = (f32[224,128]{1,0:T(8,128)}, f32[224,128]{1,0:T(8,128)S(1)}, u32[]{:S(2)}, u32[]{:S(2)}) collective-permute-start(f32[224,128]{1,0:T(8,128)} %get-tuple-element.223), channel_id=1, source_target_pairs={{0,4},{1,5},{2,6},{3,7},{8,12},{9,13},{10,14},{11,15},{16,20},{17,... | collective-permute-start | bytes 344072 | tf_op jit(solution)/shard_map/ppermute | solution.py:20
  110.9 3.5 %collective-permute-start.11 = (f32[224,128]{1,0:T(8,128)}, f32[224,128]{1,0:T(8,128)S(1)}, u32[]{:S(2)}, u32[]{:S(2)}) collective-permute-start(f32[224,128]{1,0:T(8,128)} %get-tuple-element.204), channel_id=1, source_target_pairs={{1,0},{2,1},{3,2},{5,4},{6,5},{7,6},{9,8},{10,9},{11,10},{13,12},{... | collective-permute-start | bytes 344072 | tf_op jit(solution)/shard_map/ppermute | solution.py:20
  114.4 3.5 %collective-permute-start.10 = (f32[224,128]{1,0:T(8,128)}, f32[224,128]{1,0:T(8,128)S(1)}, u32[]{:S(2)}, u32[]{:S(2)}) collective-permute-start(f32[224,128]{1,0:T(8,128)} %get-tuple-element.205), channel_id=1, source_target_pairs={{0,1},{1,2},{2,3},{4,5},{5,6},{6,7},{8,9},{9,10},{10,11},{12,13},{... | collective-permute-start | bytes 344072 | tf_op jit(solution)/shard_map/ppermute | solution.py:20
  125.6 4.5 %collective-permute-done.13 = f32[224,128]{1,0:T(8,128)S(1)} collective-permute-done((f32[224,128]{1,0:T(8,128)S(1)}, f32[224,128]{1,0:T(8,128)S(1)}, u32[]{:S(2)}, u32[]{:S(2)}) %collective-permute-start.13) | collective-permute-done | bytes 114720 | tf_op jit(solution)/shard_map/ppermute | solution.py:20
  130.2 3.4 %collective-permute-start.12 = (f32[224,128]{1,0:T(8,128)S(1)}, f32[224,128]{1,0:T(8,128)S(1)}, u32[]{:S(2)}, u32[]{:S(2)}) collective-permute-start(f32[224,128]{1,0:T(8,128)S(1)} %pad_maximum_fusion.4), channel_id=1, source_target_pairs={{0,8},{8,16},{16,24},{1,9},{9,17},{17,25},{2,10},{10,18},{18,26},{... | collective-permute-start | bytes 344072 | tf_op jit(solution)/shard_map/ppermute | solution.py:20
  133.5 2.6 collective-permute-done.12
  137.4 4.0 %collective-permute-start.14 = (f32[224,128]{1,0:T(8,128)S(1)}, f32[224,128]{1,0:T(8,128)S(1)}, u32[]{:S(2)}, u32[]{:S(2)}) collective-permute-start(f32[224,128]{1,0:T(8,128)S(1)} %get-tuple-element.199), channel_id=1, source_target_pairs={{0,4},{1,5},{2,6},{3,7},{8,12},{9,13},{10,14},{11,15},{16,20},{17,... | collective-permute-start | bytes 344072 | tf_op jit(solution)/shard_map/ppermute | solution.py:20
  143.6 3.1 %collective-permute-start.17 = (f32[224,128]{1,0:T(8,128)S(1)}, f32[224,128]{1,0:T(8,128)S(1)}, u32[]{:S(2)}, u32[]{:S(2)}) collective-permute-start(f32[224,128]{1,0:T(8,128)S(1)} %get-tuple-element.180), channel_id=1, source_target_pairs={{1,0},{2,1},{3,2},{5,4},{6,5},{7,6},{9,8},{10,9},{11,10},{13,12},{... | collective-permute-start | bytes 344072 | tf_op jit(solution)/shard_map/ppermute | solution.py:20
  146.7 5.0 %collective-permute-start.16 = (f32[224,128]{1,0:T(8,128)S(1)}, f32[224,128]{1,0:T(8,128)S(1)}, u32[]{:S(2)}, u32[]{:S(2)}) collective-permute-start(f32[224,128]{1,0:T(8,128)S(1)} %get-tuple-element.181), channel_id=1, source_target_pairs={{0,1},{1,2},{2,3},{4,5},{5,6},{6,7},{8,9},{9,10},{10,11},{12,13},{... | collective-permute-start | bytes 344072 | tf_op jit(solution)/shard_map/ppermute | solution.py:20
  154.5 6.0 %all-gather.2 = f32[4,6,128]{2,1,0:T(8,128)S(1)} all-gather(f32[1,6,128]{2,1,0:T(8,128)S(1)} %convolution_bitcast_fusion.1), channel_id=1, replica_groups=mesh['gx'=4,'gy'=2,'gz'=4] {'gz'}, dimensions={0}, use_global_device_ids=true | all-gather | bytes 15360 | tf_op jit(solution)/shard_map/all_gather | solution.py:73
  162.7 6.1 %collective-permute-done.19 = f32[224,128]{1,0:T(8,128)S(1)} collective-permute-done((f32[224,128]{1,0:T(8,128)S(1)}, f32[224,128]{1,0:T(8,128)S(1)}, u32[]{:S(2)}, u32[]{:S(2)}) %collective-permute-start.19) | collective-permute-done | bytes 114720 | tf_op jit(solution)/shard_map/ppermute | solution.py:20
  168.8 3.2 %collective-permute-start.18 = (f32[224,128]{1,0:T(8,128)S(1)}, f32[224,128]{1,0:T(8,128)S(1)}, u32[]{:S(2)}, u32[]{:S(2)}) collective-permute-start(f32[224,128]{1,0:T(8,128)S(1)} %pad_maximum_fusion.6), channel_id=1, source_target_pairs={{0,8},{8,16},{16,24},{1,9},{9,17},{17,25},{2,10},{10,18},{18,26},{... | collective-permute-start | bytes 344072 | tf_op jit(solution)/shard_map/ppermute | solution.py:20
  175.1 4.1 %collective-permute-start.20 = (f32[224,128]{1,0:T(8,128)S(1)}, f32[224,128]{1,0:T(8,128)S(1)}, u32[]{:S(2)}, u32[]{:S(2)}) collective-permute-start(f32[224,128]{1,0:T(8,128)S(1)} %get-tuple-element.175), channel_id=1, source_target_pairs={{0,4},{1,5},{2,6},{3,7},{8,12},{9,13},{10,14},{11,15},{16,20},{17,... | collective-permute-start | bytes 344072 | tf_op jit(solution)/shard_map/ppermute | solution.py:20
  181.0 4.8 %collective-permute-start.23 = (f32[224,128]{1,0:T(8,128)S(1)}, f32[224,128]{1,0:T(8,128)S(1)}, u32[]{:S(2)}, u32[]{:S(2)}) collective-permute-start(f32[224,128]{1,0:T(8,128)S(1)} %get-tuple-element.156), channel_id=1, source_target_pairs={{1,0},{2,1},{3,2},{5,4},{6,5},{7,6},{9,8},{10,9},{11,10},{13,12},{... | collective-permute-start | bytes 344072 | tf_op jit(solution)/shard_map/ppermute | solution.py:20
  185.8 3.5 %collective-permute-start.22 = (f32[224,128]{1,0:T(8,128)S(1)}, f32[224,128]{1,0:T(8,128)S(1)}, u32[]{:S(2)}, u32[]{:S(2)}) collective-permute-start(f32[224,128]{1,0:T(8,128)S(1)} %get-tuple-element.157), channel_id=1, source_target_pairs={{0,1},{1,2},{2,3},{4,5},{5,6},{6,7},{8,9},{9,10},{10,11},{12,13},{... | collective-permute-start | bytes 344072 | tf_op jit(solution)/shard_map/ppermute | solution.py:20
  193.9 4.9 %collective-permute-done.25 = f32[224,128]{1,0:T(8,128)S(1)} collective-permute-done((f32[224,128]{1,0:T(8,128)S(1)}, f32[224,128]{1,0:T(8,128)S(1)}, u32[]{:S(2)}, u32[]{:S(2)}) %collective-permute-start.25) | collective-permute-done | bytes 114720 | tf_op jit(solution)/shard_map/ppermute | solution.py:20
  198.8 3.4 %collective-permute-start.24 = (f32[224,128]{1,0:T(8,128)S(1)}, f32[224,128]{1,0:T(8,128)S(1)}, u32[]{:S(2)}, u32[]{:S(2)}) collective-permute-start(f32[224,128]{1,0:T(8,128)S(1)} %pad_maximum_fusion.8), channel_id=1, source_target_pairs={{0,8},{8,16},{16,24},{1,9},{9,17},{17,25},{2,10},{10,18},{18,26},{... | collective-permute-start | bytes 344072 | tf_op jit(solution)/shard_map/ppermute | solution.py:20
  202.2 2.7 collective-permute-done.24
  206.2 4.2 %collective-permute-start.26 = (f32[224,128]{1,0:T(8,128)S(1)}, f32[224,128]{1,0:T(8,128)S(1)}, u32[]{:S(2)}, u32[]{:S(2)}) collective-permute-start(f32[224,128]{1,0:T(8,128)S(1)} %get-tuple-element.151), channel_id=1, source_target_pairs={{0,4},{1,5},{2,6},{3,7},{8,12},{9,13},{10,14},{11,15},{16,20},{17,... | collective-permute-start | bytes 344072 | tf_op jit(solution)/shard_map/ppermute | solution.py:20
  212.5 3.1 %collective-permute-start.29 = (f32[224,128]{1,0:T(8,128)S(1)}, f32[224,128]{1,0:T(8,128)S(1)}, u32[]{:S(2)}, u32[]{:S(2)}) collective-permute-start(f32[224,128]{1,0:T(8,128)S(1)} %get-tuple-element.132), channel_id=1, source_target_pairs={{1,0},{2,1},{3,2},{5,4},{6,5},{7,6},{9,8},{10,9},{11,10},{13,12},{... | collective-permute-start | bytes 344072 | tf_op jit(solution)/shard_map/ppermute | solution.py:20
  215.6 4.9 %collective-permute-start.28 = (f32[224,128]{1,0:T(8,128)S(1)}, f32[224,128]{1,0:T(8,128)S(1)}, u32[]{:S(2)}, u32[]{:S(2)}) collective-permute-start(f32[224,128]{1,0:T(8,128)S(1)} %get-tuple-element.133), channel_id=1, source_target_pairs={{0,1},{1,2},{2,3},{4,5},{5,6},{6,7},{8,9},{9,10},{10,11},{12,13},{... | collective-permute-start | bytes 344072 | tf_op jit(solution)/shard_map/ppermute | solution.py:20
  223.2 6.0 %all-gather.3 = f32[4,6,128]{2,1,0:T(8,128)S(1)} all-gather(f32[1,6,128]{2,1,0:T(8,128)S(1)} %convolution_bitcast_fusion), channel_id=1, replica_groups=mesh['gx'=4,'gy'=2,'gz'=4] {'gz'}, dimensions={0}, use_global_device_ids=true | all-gather | bytes 15360 | tf_op jit(solution)/shard_map/all_gather | solution.py:73
  231.3 6.1 %collective-permute-done.31 = f32[224,128]{1,0:T(8,128)S(1)} collective-permute-done((f32[224,128]{1,0:T(8,128)S(1)}, f32[224,128]{1,0:T(8,128)S(1)}, u32[]{:S(2)}, u32[]{:S(2)}) %collective-permute-start.31) | collective-permute-done | bytes 114720 | tf_op jit(solution)/shard_map/ppermute | solution.py:20
  237.5 3.0 %collective-permute-start.30 = (f32[224,128]{1,0:T(8,128)S(1)}, f32[224,128]{1,0:T(8,128)S(1)}, u32[]{:S(2)}, u32[]{:S(2)}) collective-permute-start(f32[224,128]{1,0:T(8,128)S(1)} %pad_maximum_fusion.10), channel_id=1, source_target_pairs={{0,8},{8,16},{16,24},{1,9},{9,17},{17,25},{2,10},{10,18},{18,26},{... | collective-permute-start | bytes 344072 | tf_op jit(solution)/shard_map/ppermute | solution.py:20
  243.6 4.1 %collective-permute-start.32 = (f32[224,128]{1,0:T(8,128)S(1)}, f32[224,128]{1,0:T(8,128)S(1)}, u32[]{:S(2)}, u32[]{:S(2)}) collective-permute-start(f32[224,128]{1,0:T(8,128)S(1)} %get-tuple-element.127), channel_id=1, source_target_pairs={{0,4},{1,5},{2,6},{3,7},{8,12},{9,13},{10,14},{11,15},{16,20},{17,... | collective-permute-start | bytes 344072 | tf_op jit(solution)/shard_map/ppermute | solution.py:20
  249.5 4.8 %collective-permute-start.35 = (f32[224,128]{1,0:T(8,128)S(1)}, f32[224,128]{1,0:T(8,128)S(1)}, u32[]{:S(2)}, u32[]{:S(2)}) collective-permute-start(f32[224,128]{1,0:T(8,128)S(1)} %get-tuple-element.108), channel_id=1, source_target_pairs={{1,0},{2,1},{3,2},{5,4},{6,5},{7,6},{9,8},{10,9},{11,10},{13,12},{... | collective-permute-start | bytes 344072 | tf_op jit(solution)/shard_map/ppermute | solution.py:20
  254.4 3.5 %collective-permute-start.34 = (f32[224,128]{1,0:T(8,128)S(1)}, f32[224,128]{1,0:T(8,128)S(1)}, u32[]{:S(2)}, u32[]{:S(2)}) collective-permute-start(f32[224,128]{1,0:T(8,128)S(1)} %get-tuple-element.109), channel_id=1, source_target_pairs={{0,1},{1,2},{2,3},{4,5},{5,6},{6,7},{8,9},{9,10},{10,11},{12,13},{... | collective-permute-start | bytes 344072 | tf_op jit(solution)/shard_map/ppermute | solution.py:20
  262.5 4.9 %collective-permute-done.37 = f32[224,128]{1,0:T(8,128)S(1)} collective-permute-done((f32[224,128]{1,0:T(8,128)S(1)}, f32[224,128]{1,0:T(8,128)S(1)}, u32[]{:S(2)}, u32[]{:S(2)}) %collective-permute-start.37) | collective-permute-done | bytes 114720 | tf_op jit(solution)/shard_map/ppermute | solution.py:20
  267.5 3.4 %collective-permute-start.36 = (f32[224,128]{1,0:T(8,128)S(1)}, f32[224,128]{1,0:T(8,128)S(1)}, u32[]{:S(2)}, u32[]{:S(2)}) collective-permute-start(f32[224,128]{1,0:T(8,128)S(1)} %pad_maximum_fusion.12), channel_id=1, source_target_pairs={{0,8},{8,16},{16,24},{1,9},{9,17},{17,25},{2,10},{10,18},{18,26},{... | collective-permute-start | bytes 344072 | tf_op jit(solution)/shard_map/ppermute | solution.py:20
  270.9 2.7 collective-permute-done.36
  274.9 4.1 %collective-permute-start.38 = (f32[224,128]{1,0:T(8,128)S(1)}, f32[224,128]{1,0:T(8,128)S(1)}, u32[]{:S(2)}, u32[]{:S(2)}) collective-permute-start(f32[224,128]{1,0:T(8,128)S(1)} %get-tuple-element.103), channel_id=1, source_target_pairs={{0,4},{1,5},{2,6},{3,7},{8,12},{9,13},{10,14},{11,15},{16,20},{17,... | collective-permute-start | bytes 344072 | tf_op jit(solution)/shard_map/ppermute | solution.py:20
  281.1 3.1 %collective-permute-start.41 = (f32[224,128]{1,0:T(8,128)S(1)}, f32[224,128]{1,0:T(8,128)S(1)}, u32[]{:S(2)}, u32[]{:S(2)}) collective-permute-start(f32[224,128]{1,0:T(8,128)S(1)} %get-tuple-element.84), channel_id=1, source_target_pairs={{1,0},{2,1},{3,2},{5,4},{6,5},{7,6},{9,8},{10,9},{11,10},{13,12},{... | collective-permute-start | bytes 344072 | tf_op jit(solution)/shard_map/ppermute | solution.py:20
  284.2 4.9 %collective-permute-start.40 = (f32[224,128]{1,0:T(8,128)S(1)}, f32[224,128]{1,0:T(8,128)S(1)}, u32[]{:S(2)}, u32[]{:S(2)}) collective-permute-start(f32[224,128]{1,0:T(8,128)S(1)} %get-tuple-element.85), channel_id=1, source_target_pairs={{0,1},{1,2},{2,3},{4,5},{5,6},{6,7},{8,9},{9,10},{10,11},{12,13},{... | collective-permute-start | bytes 344072 | tf_op jit(solution)/shard_map/ppermute | solution.py:20
  291.5 4.0 %gather_fusion.5 = f32[1024,128]{1,0:T(8,128)} fusion(f32[1024,128]{1,0:T(8,128)S(1)} %get-tuple-element.5, s32[1024]{0:T(1024)S(1)} %get-tuple-element.254), kind=kCustom, calls=%fused_computation.1.clone | custom fusion | bytes 1052672 | tf_op jit(solution)/shard_map/jit(_take)/gather | solution.py:137
  295.5 4.0 %gather_fusion.4 = f32[1024,128]{1,0:T(8,128)} fusion(f32[1024,128]{1,0:T(8,128)S(1)} %get-tuple-element.6, s32[1024]{0:T(1024)S(1)} %get-tuple-element.254), kind=kCustom, calls=%fused_computation.clone | custom fusion | bytes 1052672 | tf_op jit(solution)/shard_map/jit(_take)/gather | solution.py:136
  (434 shorter events, 92.6 us)
Async XLA Ops:
  0.6 69.5 %copy-start = (bf16[1,1,1,1024,1024]{4,3,2,1,0:T(8,128)(2,1)S(1)}, bf16[1,1,1,1024,1024]{4,3,2,1,0:T(8,128)(2,1)}, u32[]{:S(2)}) copy-start(bf16[1,1,1,1024,1024]{4,3,2,1,0:T(8,128)(2,1)} %param.8) | copy-start | bytes 6291460
  12.8 13.7 %collective-permute-start.1 = (f32[224,128]{1,0:T(8,128)S(1)}, f32[224,128]{1,0:T(8,128)S(1)}, u32[]{:S(2)}, u32[]{:S(2)}) collective-permute-start(f32[224,128]{1,0:T(8,128)S(1)} %pad_maximum_fusion.1), channel_id=1, source_target_pairs={{8,0},{16,8},{24,16},{9,1},{17,9},{25,17},{10,2},{18,10},{26,18},{... | collective-permute-start | bytes 344072 | tf_op jit(solution)/shard_map/ppermute | solution.py:20
  28.5 6.1 %collective-permute-start = (f32[224,128]{1,0:T(8,128)S(1)}, f32[224,128]{1,0:T(8,128)S(1)}, u32[]{:S(2)}, u32[]{:S(2)}) collective-permute-start(f32[224,128]{1,0:T(8,128)S(1)} %pad_maximum_fusion), channel_id=1, source_target_pairs={{0,8},{8,16},{16,24},{1,9},{9,17},{17,25},{2,10},{10,18},{18,26},{... | collective-permute-start | bytes 344072 | tf_op jit(solution)/shard_map/ppermute | solution.py:20
  36.5 5.7 %collective-permute-start.3 = (f32[224,128]{1,0:T(8,128)}, f32[224,128]{1,0:T(8,128)S(1)}, u32[]{:S(2)}, u32[]{:S(2)}) collective-permute-start(f32[224,128]{1,0:T(8,128)} %get-tuple-element.246), channel_id=1, source_target_pairs={{4,0},{5,1},{6,2},{7,3},{12,8},{13,9},{14,10},{15,11},{20,16},{21,... | collective-permute-start | bytes 344072 | tf_op jit(solution)/shard_map/ppermute | solution.py:20
  37.8 6.1 %collective-permute-start.2 = (f32[224,128]{1,0:T(8,128)}, f32[224,128]{1,0:T(8,128)S(1)}, u32[]{:S(2)}, u32[]{:S(2)}) collective-permute-start(f32[224,128]{1,0:T(8,128)} %get-tuple-element.247), channel_id=1, source_target_pairs={{0,4},{1,5},{2,6},{3,7},{8,12},{9,13},{10,14},{11,15},{16,20},{17,... | collective-permute-start | bytes 344072 | tf_op jit(solution)/shard_map/ppermute | solution.py:20
  47.4 9.9 %collective-permute-start.5 = (f32[224,128]{1,0:T(8,128)}, f32[224,128]{1,0:T(8,128)S(1)}, u32[]{:S(2)}, u32[]{:S(2)}) collective-permute-start(f32[224,128]{1,0:T(8,128)} %get-tuple-element.228), channel_id=1, source_target_pairs={{1,0},{2,1},{3,2},{5,4},{6,5},{7,6},{9,8},{10,9},{11,10},{13,12},{... | collective-permute-start | bytes 344072 | tf_op jit(solution)/shard_map/ppermute | solution.py:20
  52.8 4.6 %collective-permute-start.4 = (f32[224,128]{1,0:T(8,128)}, f32[224,128]{1,0:T(8,128)S(1)}, u32[]{:S(2)}, u32[]{:S(2)}) collective-permute-start(f32[224,128]{1,0:T(8,128)} %get-tuple-element.229), channel_id=1, source_target_pairs={{0,1},{1,2},{2,3},{4,5},{5,6},{6,7},{8,9},{9,10},{10,11},{12,13},{... | collective-permute-start | bytes 344072 | tf_op jit(solution)/shard_map/ppermute | solution.py:20
  57.6 63.4 %copy-start.1 = (f32[1024,128]{1,0:T(8,128)}, f32[1024,128]{1,0:T(8,128)S(1)}, u32[]{:S(2)}) copy-start(f32[1024,128]{1,0:T(8,128)S(1)} %constant_dynamic-update-slice_fusion.30) | copy-start | bytes 1572868
  68.8 7.5 %collective-permute-start.7 = (f32[224,128]{1,0:T(8,128)S(1)}, f32[224,128]{1,0:T(8,128)S(1)}, u32[]{:S(2)}, u32[]{:S(2)}) collective-permute-start(f32[224,128]{1,0:T(8,128)S(1)} %pad_maximum_fusion.3), channel_id=1, source_target_pairs={{8,0},{16,8},{24,16},{9,1},{17,9},{25,17},{10,2},{18,10},{26,18},{... | collective-permute-start | bytes 344072 | tf_op jit(solution)/shard_map/ppermute | solution.py:20
  78.3 18.9 %collective-permute-start.6 = (f32[224,128]{1,0:T(8,128)S(1)}, f32[224,128]{1,0:T(8,128)S(1)}, u32[]{:S(2)}, u32[]{:S(2)}) collective-permute-start(f32[224,128]{1,0:T(8,128)S(1)} %pad_maximum_fusion.2), channel_id=1, source_target_pairs={{0,8},{8,16},{16,24},{1,9},{9,17},{17,25},{2,10},{10,18},{18,26},{... | collective-permute-start | bytes 344072 | tf_op jit(solution)/shard_map/ppermute | solution.py:20
  99.9 6.3 %collective-permute-start.9 = (f32[224,128]{1,0:T(8,128)}, f32[224,128]{1,0:T(8,128)S(1)}, u32[]{:S(2)}, u32[]{:S(2)}) collective-permute-start(f32[224,128]{1,0:T(8,128)} %get-tuple-element.222), channel_id=1, source_target_pairs={{4,0},{5,1},{6,2},{7,3},{12,8},{13,9},{14,10},{15,11},{20,16},{21,... | collective-permute-start | bytes 344072 | tf_op jit(solution)/shard_map/ppermute | solution.py:20
  101.2 6.1 %collective-permute-start.8 = (f32[224,128]{1,0:T(8,128)}, f32[224,128]{1,0:T(8,128)S(1)}, u32[]{:S(2)}, u32[]{:S(2)}) collective-permute-start(f32[224,128]{1,0:T(8,128)} %get-tuple-element.223), channel_id=1, source_target_pairs={{0,4},{1,5},{2,6},{3,7},{8,12},{9,13},{10,14},{11,15},{16,20},{17,... | collective-permute-start | bytes 344072 | tf_op jit(solution)/shard_map/ppermute | solution.py:20
  110.9 9.1 %collective-permute-start.11 = (f32[224,128]{1,0:T(8,128)}, f32[224,128]{1,0:T(8,128)S(1)}, u32[]{:S(2)}, u32[]{:S(2)}) collective-permute-start(f32[224,128]{1,0:T(8,128)} %get-tuple-element.204), channel_id=1, source_target_pairs={{1,0},{2,1},{3,2},{5,4},{6,5},{7,6},{9,8},{10,9},{11,10},{13,12},{... | collective-permute-start | bytes 344072 | tf_op jit(solution)/shard_map/ppermute | solution.py:20
  114.4 5.6 %collective-permute-start.10 = (f32[224,128]{1,0:T(8,128)}, f32[224,128]{1,0:T(8,128)S(1)}, u32[]{:S(2)}, u32[]{:S(2)}) collective-permute-start(f32[224,128]{1,0:T(8,128)} %get-tuple-element.205), channel_id=1, source_target_pairs={{0,1},{1,2},{2,3},{4,5},{5,6},{6,7},{8,9},{9,10},{10,11},{12,13},{... | collective-permute-start | bytes 344072 | tf_op jit(solution)/shard_map/ppermute | solution.py:20
  124.2 5.9 %collective-permute-start.13 = (f32[224,128]{1,0:T(8,128)S(1)}, f32[224,128]{1,0:T(8,128)S(1)}, u32[]{:S(2)}, u32[]{:S(2)}) collective-permute-start(f32[224,128]{1,0:T(8,128)S(1)} %pad_maximum_fusion.5), channel_id=1, source_target_pairs={{8,0},{16,8},{24,16},{9,1},{17,9},{25,17},{10,2},{18,10},{26,18},{... | collective-permute-start | bytes 344072 | tf_op jit(solution)/shard_map/ppermute | solution.py:20
  130.2 5.9 %collective-permute-start.12 = (f32[224,128]{1,0:T(8,128)S(1)}, f32[224,128]{1,0:T(8,128)S(1)}, u32[]{:S(2)}, u32[]{:S(2)}) collective-permute-start(f32[224,128]{1,0:T(8,128)S(1)} %pad_maximum_fusion.4), channel_id=1, source_target_pairs={{0,8},{8,16},{16,24},{1,9},{9,17},{17,25},{2,10},{10,18},{18,26},{... | collective-permute-start | bytes 344072 | tf_op jit(solution)/shard_map/ppermute | solution.py:20
  136.1 6.6 %collective-permute-start.15 = (f32[224,128]{1,0:T(8,128)S(1)}, f32[224,128]{1,0:T(8,128)S(1)}, u32[]{:S(2)}, u32[]{:S(2)}) collective-permute-start(f32[224,128]{1,0:T(8,128)S(1)} %get-tuple-element.198), channel_id=1, source_target_pairs={{4,0},{5,1},{6,2},{7,3},{12,8},{13,9},{14,10},{15,11},{20,16},{21,... | collective-permute-start | bytes 344072 | tf_op jit(solution)/shard_map/ppermute | solution.py:20
  137.4 6.2 %collective-permute-start.14 = (f32[224,128]{1,0:T(8,128)S(1)}, f32[224,128]{1,0:T(8,128)S(1)}, u32[]{:S(2)}, u32[]{:S(2)}) collective-permute-start(f32[224,128]{1,0:T(8,128)S(1)} %get-tuple-element.199), channel_id=1, source_target_pairs={{0,4},{1,5},{2,6},{3,7},{8,12},{9,13},{10,14},{11,15},{16,20},{17,... | collective-permute-start | bytes 344072 | tf_op jit(solution)/shard_map/ppermute | solution.py:20
  143.6 9.9 %collective-permute-start.17 = (f32[224,128]{1,0:T(8,128)S(1)}, f32[224,128]{1,0:T(8,128)S(1)}, u32[]{:S(2)}, u32[]{:S(2)}) collective-permute-start(f32[224,128]{1,0:T(8,128)S(1)} %get-tuple-element.180), channel_id=1, source_target_pairs={{1,0},{2,1},{3,2},{5,4},{6,5},{7,6},{9,8},{10,9},{11,10},{13,12},{... | collective-permute-start | bytes 344072 | tf_op jit(solution)/shard_map/ppermute | solution.py:20
  146.7 6.8 %collective-permute-start.16 = (f32[224,128]{1,0:T(8,128)S(1)}, f32[224,128]{1,0:T(8,128)S(1)}, u32[]{:S(2)}, u32[]{:S(2)}) collective-permute-start(f32[224,128]{1,0:T(8,128)S(1)} %get-tuple-element.181), channel_id=1, source_target_pairs={{0,1},{1,2},{2,3},{4,5},{5,6},{6,7},{8,9},{9,10},{10,11},{12,13},{... | collective-permute-start | bytes 344072 | tf_op jit(solution)/shard_map/ppermute | solution.py:20
  154.5 36.9 %copy-start.4 = (f32[1024,128]{1,0:T(8,128)S(1)}, f32[1024,128]{1,0:T(8,128)}, u32[]{:S(2)}) copy-start(f32[1024,128]{1,0:T(8,128)} %copy-done.3) | copy-start | bytes 1572868
  161.4 7.4 %collective-permute-start.19 = (f32[224,128]{1,0:T(8,128)S(1)}, f32[224,128]{1,0:T(8,128)S(1)}, u32[]{:S(2)}, u32[]{:S(2)}) collective-permute-start(f32[224,128]{1,0:T(8,128)S(1)} %pad_maximum_fusion.7), channel_id=1, source_target_pairs={{8,0},{16,8},{24,16},{9,1},{17,9},{25,17},{10,2},{18,10},{26,18},{... | collective-permute-start | bytes 344072 | tf_op jit(solution)/shard_map/ppermute | solution.py:20
  168.8 5.0 %collective-permute-start.18 = (f32[224,128]{1,0:T(8,128)S(1)}, f32[224,128]{1,0:T(8,128)S(1)}, u32[]{:S(2)}, u32[]{:S(2)}) collective-permute-start(f32[224,128]{1,0:T(8,128)S(1)} %pad_maximum_fusion.6), channel_id=1, source_target_pairs={{0,8},{8,16},{16,24},{1,9},{9,17},{17,25},{2,10},{10,18},{18,26},{... | collective-permute-start | bytes 344072 | tf_op jit(solution)/shard_map/ppermute | solution.py:20
  173.8 5.6 %collective-permute-start.21 = (f32[224,128]{1,0:T(8,128)S(1)}, f32[224,128]{1,0:T(8,128)S(1)}, u32[]{:S(2)}, u32[]{:S(2)}) collective-permute-start(f32[224,128]{1,0:T(8,128)S(1)} %get-tuple-element.174), channel_id=1, source_target_pairs={{4,0},{5,1},{6,2},{7,3},{12,8},{13,9},{14,10},{15,11},{20,16},{21,... | collective-permute-start | bytes 344072 | tf_op jit(solution)/shard_map/ppermute | solution.py:20
  175.1 5.8 %collective-permute-start.20 = (f32[224,128]{1,0:T(8,128)S(1)}, f32[224,128]{1,0:T(8,128)S(1)}, u32[]{:S(2)}, u32[]{:S(2)}) collective-permute-start(f32[224,128]{1,0:T(8,128)S(1)} %get-tuple-element.175), channel_id=1, source_target_pairs={{0,4},{1,5},{2,6},{3,7},{8,12},{9,13},{10,14},{11,15},{16,20},{17,... | collective-permute-start | bytes 344072 | tf_op jit(solution)/shard_map/ppermute | solution.py:20
  181.0 10.1 %collective-permute-start.23 = (f32[224,128]{1,0:T(8,128)S(1)}, f32[224,128]{1,0:T(8,128)S(1)}, u32[]{:S(2)}, u32[]{:S(2)}) collective-permute-start(f32[224,128]{1,0:T(8,128)S(1)} %get-tuple-element.156), channel_id=1, source_target_pairs={{1,0},{2,1},{3,2},{5,4},{6,5},{7,6},{9,8},{10,9},{11,10},{13,12},{... | collective-permute-start | bytes 344072 | tf_op jit(solution)/shard_map/ppermute | solution.py:20
  185.8 5.2 %collective-permute-start.22 = (f32[224,128]{1,0:T(8,128)S(1)}, f32[224,128]{1,0:T(8,128)S(1)}, u32[]{:S(2)}, u32[]{:S(2)}) collective-permute-start(f32[224,128]{1,0:T(8,128)S(1)} %get-tuple-element.157), channel_id=1, source_target_pairs={{0,1},{1,2},{2,3},{4,5},{5,6},{6,7},{8,9},{9,10},{10,11},{12,13},{... | collective-permute-start | bytes 344072 | tf_op jit(solution)/shard_map/ppermute | solution.py:20
  192.6 6.2 %collective-permute-start.25 = (f32[224,128]{1,0:T(8,128)S(1)}, f32[224,128]{1,0:T(8,128)S(1)}, u32[]{:S(2)}, u32[]{:S(2)}) collective-permute-start(f32[224,128]{1,0:T(8,128)S(1)} %pad_maximum_fusion.9), channel_id=1, source_target_pairs={{8,0},{16,8},{24,16},{9,1},{17,9},{25,17},{10,2},{18,10},{26,18},{... | collective-permute-start | bytes 344072 | tf_op jit(solution)/shard_map/ppermute | solution.py:20
  198.8 6.1 %collective-permute-start.24 = (f32[224,128]{1,0:T(8,128)S(1)}, f32[224,128]{1,0:T(8,128)S(1)}, u32[]{:S(2)}, u32[]{:S(2)}) collective-permute-start(f32[224,128]{1,0:T(8,128)S(1)} %pad_maximum_fusion.8), channel_id=1, source_target_pairs={{0,8},{8,16},{16,24},{1,9},{9,17},{17,25},{2,10},{10,18},{18,26},{... | collective-permute-start | bytes 344072 | tf_op jit(solution)/shard_map/ppermute | solution.py:20
  204.9 6.6 %collective-permute-start.27 = (f32[224,128]{1,0:T(8,128)S(1)}, f32[224,128]{1,0:T(8,128)S(1)}, u32[]{:S(2)}, u32[]{:S(2)}) collective-permute-start(f32[224,128]{1,0:T(8,128)S(1)} %get-tuple-element.150), channel_id=1, source_target_pairs={{4,0},{5,1},{6,2},{7,3},{12,8},{13,9},{14,10},{15,11},{20,16},{21,... | collective-permute-start | bytes 344072 | tf_op jit(solution)/shard_map/ppermute | solution.py:20
  206.2 6.2 %collective-permute-start.26 = (f32[224,128]{1,0:T(8,128)S(1)}, f32[224,128]{1,0:T(8,128)S(1)}, u32[]{:S(2)}, u32[]{:S(2)}) collective-permute-start(f32[224,128]{1,0:T(8,128)S(1)} %get-tuple-element.151), channel_id=1, source_target_pairs={{0,4},{1,5},{2,6},{3,7},{8,12},{9,13},{10,14},{11,15},{16,20},{17,... | collective-permute-start | bytes 344072 | tf_op jit(solution)/shard_map/ppermute | solution.py:20
  212.5 9.8 %collective-permute-start.29 = (f32[224,128]{1,0:T(8,128)S(1)}, f32[224,128]{1,0:T(8,128)S(1)}, u32[]{:S(2)}, u32[]{:S(2)}) collective-permute-start(f32[224,128]{1,0:T(8,128)S(1)} %get-tuple-element.132), channel_id=1, source_target_pairs={{1,0},{2,1},{3,2},{5,4},{6,5},{7,6},{9,8},{10,9},{11,10},{13,12},{... | collective-permute-start | bytes 344072 | tf_op jit(solution)/shard_map/ppermute | solution.py:20
  215.6 6.7 %collective-permute-start.28 = (f32[224,128]{1,0:T(8,128)S(1)}, f32[224,128]{1,0:T(8,128)S(1)}, u32[]{:S(2)}, u32[]{:S(2)}) collective-permute-start(f32[224,128]{1,0:T(8,128)S(1)} %get-tuple-element.133), channel_id=1, source_target_pairs={{0,1},{1,2},{2,3},{4,5},{5,6},{6,7},{8,9},{9,10},{10,11},{12,13},{... | collective-permute-start | bytes 344072 | tf_op jit(solution)/shard_map/ppermute | solution.py:20
  222.7 37.2 %copy-start.6 = (f32[1024,128]{1,0:T(8,128)}, f32[1024,128]{1,0:T(8,128)S(1)}, u32[]{:S(2)}) copy-start(f32[1024,128]{1,0:T(8,128)S(1)} %add_subtract_fusion.1) | copy-start | bytes 1572868
  223.2 36.7 %copy-start.12 = (f32[1024,128]{1,0:T(8,128)S(1)}, f32[1024,128]{1,0:T(8,128)}, u32[]{:S(2)}) copy-start(f32[1024,128]{1,0:T(8,128)} %copy-done.11) | copy-start | bytes 1572868
  229.2 30.7 %copy-start.10 = (bf16[1024,1024]{1,0:T(8,128)(2,1)S(1)}, bf16[1024,1024]{1,0:T(8,128)(2,1)}, u32[]{:S(2)}) copy-start(bf16[1024,1024]{1,0:T(8,128)(2,1)} %gather_fusion.3) | copy-start | bytes 6291460
  230.0 7.4 %collective-permute-start.31 = (f32[224,128]{1,0:T(8,128)S(1)}, f32[224,128]{1,0:T(8,128)S(1)}, u32[]{:S(2)}, u32[]{:S(2)}) collective-permute-start(f32[224,128]{1,0:T(8,128)S(1)} %pad_maximum_fusion.11), channel_id=1, source_target_pairs={{8,0},{16,8},{24,16},{9,1},{17,9},{25,17},{10,2},{18,10},{26,18},{... | collective-permute-start | bytes 344072 | tf_op jit(solution)/shard_map/ppermute | solution.py:20
  237.5 4.8 %collective-permute-start.30 = (f32[224,128]{1,0:T(8,128)S(1)}, f32[224,128]{1,0:T(8,128)S(1)}, u32[]{:S(2)}, u32[]{:S(2)}) collective-permute-start(f32[224,128]{1,0:T(8,128)S(1)} %pad_maximum_fusion.10), channel_id=1, source_target_pairs={{0,8},{8,16},{16,24},{1,9},{9,17},{17,25},{2,10},{10,18},{18,26},{... | collective-permute-start | bytes 344072 | tf_op jit(solution)/shard_map/ppermute | solution.py:20
  242.3 5.6 %collective-permute-start.33 = (f32[224,128]{1,0:T(8,128)S(1)}, f32[224,128]{1,0:T(8,128)S(1)}, u32[]{:S(2)}, u32[]{:S(2)}) collective-permute-start(f32[224,128]{1,0:T(8,128)S(1)} %get-tuple-element.126), channel_id=1, source_target_pairs={{4,0},{5,1},{6,2},{7,3},{12,8},{13,9},{14,10},{15,11},{20,16},{21,... | collective-permute-start | bytes 344072 | tf_op jit(solution)/shard_map/ppermute | solution.py:20
  243.6 5.8 %collective-permute-start.32 = (f32[224,128]{1,0:T(8,128)S(1)}, f32[224,128]{1,0:T(8,128)S(1)}, u32[]{:S(2)}, u32[]{:S(2)}) collective-permute-start(f32[224,128]{1,0:T(8,128)S(1)} %get-tuple-element.127), channel_id=1, source_target_pairs={{0,4},{1,5},{2,6},{3,7},{8,12},{9,13},{10,14},{11,15},{16,20},{17,... | collective-permute-start | bytes 344072 | tf_op jit(solution)/shard_map/ppermute | solution.py:20
  249.5 10.1 %collective-permute-start.35 = (f32[224,128]{1,0:T(8,128)S(1)}, f32[224,128]{1,0:T(8,128)S(1)}, u32[]{:S(2)}, u32[]{:S(2)}) collective-permute-start(f32[224,128]{1,0:T(8,128)S(1)} %get-tuple-element.108), channel_id=1, source_target_pairs={{1,0},{2,1},{3,2},{5,4},{6,5},{7,6},{9,8},{10,9},{11,10},{13,12},{... | collective-permute-start | bytes 344072 | tf_op jit(solution)/shard_map/ppermute | solution.py:20
  254.4 5.2 %collective-permute-start.34 = (f32[224,128]{1,0:T(8,128)S(1)}, f32[224,128]{1,0:T(8,128)S(1)}, u32[]{:S(2)}, u32[]{:S(2)}) collective-permute-start(f32[224,128]{1,0:T(8,128)S(1)} %get-tuple-element.109), channel_id=1, source_target_pairs={{0,1},{1,2},{2,3},{4,5},{5,6},{6,7},{8,9},{9,10},{10,11},{12,13},{... | collective-permute-start | bytes 344072 | tf_op jit(solution)/shard_map/ppermute | solution.py:20
  261.1 6.4 %collective-permute-start.37 = (f32[224,128]{1,0:T(8,128)S(1)}, f32[224,128]{1,0:T(8,128)S(1)}, u32[]{:S(2)}, u32[]{:S(2)}) collective-permute-start(f32[224,128]{1,0:T(8,128)S(1)} %pad_maximum_fusion.13), channel_id=1, source_target_pairs={{8,0},{16,8},{24,16},{9,1},{17,9},{25,17},{10,2},{18,10},{26,18},{... | collective-permute-start | bytes 344072 | tf_op jit(solution)/shard_map/ppermute | solution.py:20
  267.5 6.1 %collective-permute-start.36 = (f32[224,128]{1,0:T(8,128)S(1)}, f32[224,128]{1,0:T(8,128)S(1)}, u32[]{:S(2)}, u32[]{:S(2)}) collective-permute-start(f32[224,128]{1,0:T(8,128)S(1)} %pad_maximum_fusion.12), channel_id=1, source_target_pairs={{0,8},{8,16},{16,24},{1,9},{9,17},{17,25},{2,10},{10,18},{18,26},{... | collective-permute-start | bytes 344072 | tf_op jit(solution)/shard_map/ppermute | solution.py:20
  273.6 6.6 %collective-permute-start.39 = (f32[224,128]{1,0:T(8,128)S(1)}, f32[224,128]{1,0:T(8,128)S(1)}, u32[]{:S(2)}, u32[]{:S(2)}) collective-permute-start(f32[224,128]{1,0:T(8,128)S(1)} %get-tuple-element.102), channel_id=1, source_target_pairs={{4,0},{5,1},{6,2},{7,3},{12,8},{13,9},{14,10},{15,11},{20,16},{21,... | collective-permute-start | bytes 344072 | tf_op jit(solution)/shard_map/ppermute | solution.py:20
  274.9 6.2 %collective-permute-start.38 = (f32[224,128]{1,0:T(8,128)S(1)}, f32[224,128]{1,0:T(8,128)S(1)}, u32[]{:S(2)}, u32[]{:S(2)}) collective-permute-start(f32[224,128]{1,0:T(8,128)S(1)} %get-tuple-element.103), channel_id=1, source_target_pairs={{0,4},{1,5},{2,6},{3,7},{8,12},{9,13},{10,14},{11,15},{16,20},{17,... | collective-permute-start | bytes 344072 | tf_op jit(solution)/shard_map/ppermute | solution.py:20
  281.1 9.8 %collective-permute-start.41 = (f32[224,128]{1,0:T(8,128)S(1)}, f32[224,128]{1,0:T(8,128)S(1)}, u32[]{:S(2)}, u32[]{:S(2)}) collective-permute-start(f32[224,128]{1,0:T(8,128)S(1)} %get-tuple-element.84), channel_id=1, source_target_pairs={{1,0},{2,1},{3,2},{5,4},{6,5},{7,6},{9,8},{10,9},{11,10},{13,12},{... | collective-permute-start | bytes 344072 | tf_op jit(solution)/shard_map/ppermute | solution.py:20
  284.2 6.7 %collective-permute-start.40 = (f32[224,128]{1,0:T(8,128)S(1)}, f32[224,128]{1,0:T(8,128)S(1)}, u32[]{:S(2)}, u32[]{:S(2)}) collective-permute-start(f32[224,128]{1,0:T(8,128)S(1)} %get-tuple-element.85), channel_id=1, source_target_pairs={{0,1},{1,2},{2,3},{4,5},{5,6},{6,7},{8,9},{9,10},{10,11},{12,13},{... | collective-permute-start | bytes 344072 | tf_op jit(solution)/shard_map/ppermute | solution.py:20
  (15 other events, 224.3 us)
where the time goes:
time: 305 us; the launch traced here: 302 us
  starting transfers between devices  127 us (42%)
  waiting for transfers between devices  66 us (22%)
  local copies, waits for them, and re-layouts  58.4 us (19%)
  blocking collectives  24.2 us (8%)
  other arithmetic  14.5 us (5%)
  matrix products  8.02 us (3%)
  between operations  3.79 us (1%)
    ppermute x42, starting transfers between devices, from_behind(): return lax.ppermute(block, axis, route)  127 us
    ppermute x42, waiting for transfers between devices, from_behind(): return lax.ppermute(block, axis, route)  66 us
    unnamed x301, local copies, waits for them, and re-layouts  21.9 us
    all_gather x3, blocking collectives, coarse_amplitude(): lax.all_gather(project, 'gz', axis=0, tiled=True)  17.7 us
    gather x1, local copies, waits for them, and re-layouts, local(): jnp.take(jnp.take(dual_blocks[0, 0, 0], packing, axis=0), packing, axis=1)  7.9 us
    all_gather x1, blocking collectives, coarse_amplitude(): lax.all_gather(count_value, 'gz', axis=0, tiled=True)  6.42 us
  transfers between devices with their start and end apart: 42, of which 33 were waited for; matrix products, arithmetic and copies ran while one was open for 9% of the time, Pallas kernels for 0%

commit v1 on v0

v1 whole, which is shorter than its diff:
```python
import functools

import jax
import jax.numpy as jnp
from jax import lax
from jax.experimental import pallas as pl
from jax.experimental.pallas import tpu as pltpu
from jax.sharding import PartitionSpec as P

FACE = 128
EDGE = 16
CORNER = 8
ITERS = 3
EIG_LOW = 0.5
EIG_HIGH = 6.0

MESH = pl.DeviceIdType.MESH
LANES = 128
SUB = 8
F32 = jnp.float32
BF16 = jnp.bfloat16
HIGHEST = lax.Precision.HIGHEST


def slot_table():
    slots = []
    begin = 0
    for weight, width in ((1, FACE), (2, EDGE), (3, CORNER)):
        for a in (-1, 0, 1):
            for b in (-1, 0, 1):
                for c in (-1, 0, 1):
                    if abs(a) + abs(b) + abs(c) == weight:
                        slots.append(((a, b, c), begin, width))
                        begin += width
    return slots


SLOTS = slot_table()
BEGIN = {offset: begin for offset, begin, _ in SLOTS}
LINES = [(a, b) for a in (-1, 0, 1) for b in (-1, 0, 1)]
OWN = 4
BLOCKS = 3 * len(LINES)


def coefficients():
    center = 0.5 * (EIG_HIGH + EIG_LOW)
    half = 0.5 * (EIG_HIGH - EIG_LOW)
    pairs = [(0.0, 1.0 / center)]
    rho = half / center
    for _ in range(1, ITERS):
        following = 1.0 / (2.0 * center / half - rho)
        pairs.append((following * rho, 2.0 * following / half))
        rho = following
    return pairs


def halves(x):
    high = x.astype(BF16)
    low = (x - high.astype(F32)).astype(BF16)
    return jnp.concatenate([high, low], axis=1)


def kernel(shape, dual_ref, load_ref, order_ref, modes_ref, count_ref, inverse_ref,
           mult_out, res_out,
           perm, perm_t, half_packed, packed, image, received, own_modes, far_modes, wide,
           residual, direction, multipliers, modes_t, mode_pad,
           project_out, projects, inverses, select_pad, select_all, coarse,
           send_a, recv_a, send_m, recv_m, send_b, recv_b, send_i, recv_i):
    nx, ny, nz = shape
    ix, iy, iz = lax.axis_index("gx"), lax.axis_index("gy"), lax.axis_index("gz")
    m = dual_ref.shape[0]
    nmode = modes_ref.shape[0]
    csize = inverse_ref.shape[0]
    cwide = inverses.shape[2]
    line_rows = nz * SUB
    barrier = pltpu.get_barrier_semaphore()

    def line_exists(line):
        a, b = line
        return (ix + a >= 0) & (ix + a < nx) & (iy + b >= 0) & (iy + b < ny)

    def slot_exists(offset):
        return line_exists(offset[:2]) & (iz + offset[2] >= 0) & (iz + offset[2] < nz)

    def each_device(line_index, action):
        def step(t, carry):
            if line_index == OWN:
                @pl.when(t != iz)
                def _():
                    action(t)
            else:
                action(t)
            return carry
        lax.fori_loop(0, nz, step, 0, unroll=nz <= 4)

    for index, line in enumerate(LINES):
        @pl.when(line_exists(line))
        def _(index=index, line=line):
            def greet(t):
                pl.semaphore_signal(barrier, inc=1, device_id=(ix + line[0], iy + line[1], t),
                                    device_id_type=MESH)
            each_device(index, greet)

    def slot_copy(source, target, send, recv, number):
        offset, begin, width = SLOTS[number]
        back = (-offset[0], -offset[1], -offset[2])
        return pltpu.make_async_remote_copy(
            src_ref=source.at[pl.ds(begin, width)],
            dst_ref=target.at[pl.ds(BEGIN[back], width)],
            send_sem=send.at[number],
            recv_sem=recv.at[[s[0] for s in SLOTS].index(back)],
            device_id=(ix + offset[0], iy + offset[1], iz + offset[2]),
            device_id_type=MESH)

    def slot_arrival(target, send, recv, number):
        offset, begin, width = SLOTS[number]
        return pltpu.make_async_remote_copy(
            src_ref=target.at[pl.ds(begin, width)],
            dst_ref=target.at[pl.ds(begin, width)],
            send_sem=send.at[number], recv_sem=recv.at[number],
            device_id=(ix + offset[0], iy + offset[1], iz + offset[2]),
            device_id_type=MESH)

    def send_slots(source, target, send, recv, numbers):
        for number in numbers:
            @pl.when(slot_exists(SLOTS[number][0]))
            def _(number=number):
                slot_copy(source, target, send, recv, number).start()

    def wait_slots(source, target, send, recv):
        for number in range(len(SLOTS)):
            @pl.when(slot_exists(SLOTS[number][0]))
            def _(number=number):
                slot_arrival(target, send, recv, number).wait_recv()
                slot_copy(source, target, send, recv, number).wait_send()

    def send_blocks(phase):
        for index, line in enumerate(LINES):
            @pl.when(line_exists(line))
            def _(index=index, line=line):
                def copy(t):
                    pltpu.make_async_remote_copy(
                        src_ref=project_out.at[phase],
                        dst_ref=projects.at[phase, (8 - index) * nz + iz],
                        send_sem=send_b.at[index],
                        recv_sem=recv_b.at[phase, 8 - index],
                        device_id=(ix + line[0], iy + line[1], t),
                        device_id_type=MESH).start()
                each_device(index, copy)

    def wait_blocks(phase):
        for index, line in enumerate(LINES):
            blocks = nz - 1 if index == OWN else nz
            if blocks == 0:
                continue
            @pl.when(line_exists(line))
            def _(index=index, line=line, blocks=blocks):
                span = projects.at[phase, pl.ds(index * nz, blocks)]
                arrival = pltpu.make_async_remote_copy(
                    src_ref=span, dst_ref=span,
                    send_sem=send_b.at[index], recv_sem=recv_b.at[phase, index],
                    device_id=(ix + line[0], iy + line[1], iz), device_id_type=MESH)
                arrival.wait_recv()
                arrival.wait_send()

    def inverse_copy(index):
        line = LINES[index]
        return pltpu.make_async_remote_copy(
            src_ref=inverses.at[OWN], dst_ref=inverses.at[8 - index],
            send_sem=send_i.at[index], recv_sem=recv_i.at[8 - index],
            device_id=(ix + line[0], iy + line[1], iz), device_id_type=MESH)

    def publish(phase, block):
        project_out[phase] = block
        projects[phase, OWN * nz + iz] = block

    def project():
        both = jnp.dot(modes_t[...], halves(residual[...]), preferred_element_type=F32)
        return (both[:, :LANES] + both[:, LANES:])[:SUB]

    order_rows = jnp.broadcast_to(order_ref[...].astype(F32), (LANES, m))
    order_cols = order_rows.T
    lane = lax.broadcasted_iota(jnp.int32, (m, LANES), 1).astype(F32)
    for part in range(m // LANES):
        hit = order_cols == lane + float(part * LANES)
        perm[:, part * LANES:(part + 1) * LANES] = jnp.where(hit, 1.0, 0.0).astype(BF16)

    mode_pad[...] = jnp.zeros_like(mode_pad)
    mode_pad[pl.ds(0, nmode)] = modes_ref[...].astype(F32)
    repeated = jnp.concatenate([mode_pad[...]] * (LANES // SUB), axis=0).T.astype(BF16)
    rows = jnp.concatenate([load_ref[...], repeated], axis=1)
    both = jnp.dot(perm[...], rows, preferred_element_type=F32)
    image[...] = both[:, :LANES]
    own_modes[...] = both[:, LANES:]

    inverses[OWN] = jnp.zeros((csize, cwide), F32)
    inverses[OWN, :, pl.ds(0, csize)] = inverse_ref[...]
    publish(0, jnp.full((SUB, LANES), count_ref[0], jnp.int32).astype(F32))

    lines_x = 1 + jnp.where(ix > 0, 1, 0) + jnp.where(ix < nx - 1, 1, 0)
    lines_y = 1 + jnp.where(iy > 0, 1, 0) + jnp.where(iy < ny - 1, 1, 0)
    pl.semaphore_wait(barrier, lines_x * lines_y * nz - 1)

    every = range(len(SLOTS))
    send_slots(image, received, send_a, recv_a, every)
    send_blocks(0)
    for index, line in enumerate(LINES):
        if index != OWN:
            @pl.when(line_exists(line))
            def _(index=index):
                inverse_copy(index).start()
    send_slots(own_modes, far_modes, send_m, recv_m, every)

    for offset, begin, width in SLOTS:
        @pl.when(jnp.logical_not(slot_exists(offset)))
        def _(begin=begin, width=width):
            received[pl.ds(begin, width)] = jnp.zeros((width, LANES), F32)
            far_modes[pl.ds(begin, width)] = jnp.zeros((width, LANES), F32)
    for index, line in enumerate(LINES):
        @pl.when(jnp.logical_not(line_exists(line)))
        def _(index=index):
            projects[:, pl.ds(index * nz, nz)] = jnp.zeros((ITERS + 1, nz, SUB, LANES), F32)
            inverses[index] = jnp.zeros((csize, cwide), F32)

    modes_t[...] = own_modes[...].T[:modes_t.shape[0]].astype(BF16)
    tile = 2 * LANES
    order_row = order_ref[...]

    def transpose_tile(step, carry):
        base = pl.multiple_of(step * tile, tile)
        row = lax.broadcasted_iota(jnp.int32, (tile, m), 0) + base
        perm_t[pl.ds(base, tile)] = jnp.where(row == order_row, 1.0, 0.0).astype(BF16)
        return carry
    lax.fori_loop(0, m // tile, transpose_tile, 0)

    def first_product(step, carry):
        base = pl.multiple_of(step * tile, tile)
        half_packed[pl.ds(base, tile)] = jnp.dot(
            dual_ref[pl.ds(base, tile)], perm_t[...], preferred_element_type=F32).astype(BF16)
        return carry
    lax.fori_loop(0, m // tile, first_product, 0)

    wait_slots(image, received, send_a, recv_a)
    residual[...] = image[...] + received[...]
    wait_blocks(0)
    publish(1, project())
    send_blocks(1)

    def second_product(step, carry):
        base = pl.multiple_of(step * tile, tile)
        packed[pl.ds(base, tile)] = jnp.dot(
            perm[pl.ds(base, tile)], half_packed[...], preferred_element_type=F32).astype(BF16)
        return carry
    lax.fori_loop(0, m // tile, second_product, 0)

    select_pad[...] = jnp.zeros_like(select_pad)
    sub_index = lax.broadcasted_iota(jnp.int32, (SUB, cwide), 0).astype(F32)
    position = lax.broadcasted_iota(jnp.int32, (SUB, cwide), 1).astype(F32)
    for index in range(len(LINES)):
        start = jnp.zeros((SUB, cwide), F32)
        for t in range(nz):
            count = jnp.concatenate([projects[0, index * nz + t]] * (cwide // LANES), axis=1)
            hit = (position == start + sub_index) & (sub_index < count)
            chosen = jnp.where(hit, 1.0, 0.0)
            select_pad[index, pl.ds((t + 1) * SUB, SUB)] = chosen
            select_all[pl.ds((index * nz + t) * SUB, SUB)] = chosen
            start = start + count
    for index, line in enumerate(LINES):
        if index != OWN:
            @pl.when(line_exists(line))
            def _(index=index):
                inverse_copy(8 - index).wait_recv()
                inverse_copy(index).wait_send()
    total = coarse.shape[0] // 2
    lane_all = lax.broadcasted_iota(jnp.int32, (3 * SUB, len(LINES) * line_rows), 1)
    strips = []
    for index in range(len(LINES)):
        near = select_pad[index, pl.ds(pl.multiple_of(iz * SUB, SUB), 3 * SUB)]
        left = jnp.dot(near[:, :csize], inverses[index], precision=HIGHEST, preferred_element_type=F32)
        strip = lax.dot_general(left, select_all[...], (((1,), (1,)), ((), ())),
                                precision=HIGHEST, preferred_element_type=F32)
        inside = (lane_all >= index * line_rows) & (lane_all < (index + 1) * line_rows)
        strips.append(jnp.where(inside, strip, 0.0))
    strips.append(jnp.zeros((total - BLOCKS * SUB, len(LINES) * line_rows), F32))
    whole = jnp.concatenate(strips, axis=0)
    high = whole.astype(BF16)
    coarse[pl.ds(0, total)] = high
    coarse[pl.ds(total, total)] = (whole - high.astype(F32)).astype(BF16)

    wait_slots(own_modes, far_modes, send_m, recv_m)
    numbers = [(((o[0] + 1) * 3 + o[1] + 1) * 3 + o[2] + 1) for o, _, _ in SLOTS]
    row_block = jnp.concatenate(
        [jnp.full((SLOTS[k][2], LANES), numbers[k], jnp.int32) for k in every], axis=0)
    lane_row = lax.broadcasted_iota(jnp.int32, (m, LANES), 1)
    for part in range(total // LANES):
        block = (lane_row + part * LANES) // SUB
        value = jnp.where(block == row_block, far_modes[...],
                          jnp.where(block == BLOCKS // 2, own_modes[...], 0.0))
        wide[:, part * LANES:(part + 1) * LANES] = value.astype(BF16)

    direction[...] = jnp.zeros_like(direction)
    multipliers[...] = jnp.zeros_like(multipliers)
    faces = 6 * FACE
    pairs = coefficients()

    def iteration(step, carry):
        keep, gain = jnp.float32(pairs[0][0]), jnp.float32(pairs[0][1])
        for k in range(1, ITERS):
            keep = jnp.where(step == k, jnp.float32(pairs[k][0]), keep)
            gain = jnp.where(step == k, jnp.float32(pairs[k][1]), gain)
        wait_blocks(step + 1)
        line_projects = projects[step + 1].reshape(len(LINES) * line_rows, LANES)
        four = jnp.dot(coarse[...], halves(line_projects), preferred_element_type=F32)
        amplitude = four[:total, :LANES] + (four[:total, LANES:] + four[total:, :LANES])
        both = jnp.dot(wide[...], halves(amplitude), preferred_element_type=F32)
        corrected = residual[...] - (both[:, :LANES] + both[:, LANES:])
        now = keep * direction[...] + gain * corrected
        direction[...] = now
        multipliers[...] = multipliers[...] + now
        rounded = now.astype(BF16)
        image[pl.ds(0, faces)] = jnp.dot(packed[pl.ds(0, faces)], rounded, preferred_element_type=F32)
        send_slots(image, received, send_a, recv_a, range(6))
        image[pl.ds(faces, m - faces)] = jnp.dot(
            packed[pl.ds(faces, m - faces)], rounded, preferred_element_type=F32)
        send_slots(image, received, send_a, recv_a, range(6, len(SLOTS)))

        @pl.when(step == ITERS - 1)
        def _():
            pair = jnp.dot(perm_t[...], halves(multipliers[...]), preferred_element_type=F32)
            mult_out[...] = pair[:, :LANES] + pair[:, LANES:]

        wait_slots(image, received, send_a, recv_a)
        residual[...] = residual[...] - image[...] - received[...]

        @pl.when(step < ITERS - 1)
        def _():
            publish(step + 2, project())
            send_blocks(step + 2)
        return carry
    lax.fori_loop(0, ITERS, iteration, 0)

    pair = jnp.dot(perm_t[...], halves(residual[...]), preferred_element_type=F32)
    res_out[...] = pair[:, :LANES] + pair[:, LANES:]


def local(shape, dual_blocks, load_terms, row_order, mode_rows, mode_count, coarse_inverse):
    nz = shape[2]
    m, loads = load_terms.shape[3:]
    csize = coarse_inverse.shape[2]
    cwide = -(-csize // LANES) * LANES
    lines = len(LINES)
    line_rows = nz * SUB
    total = -(-BLOCKS * SUB // LANES) * LANES
    vmem = pl.BlockSpec(memory_space=pltpu.VMEM)
    smem = pl.BlockSpec(memory_space=pltpu.SMEM)
    rows = pltpu.VMEM((m, loads), F32)
    square = pltpu.VMEM((m, m), BF16)
    dma = pltpu.SemaphoreType.DMA
    slots = len(SLOTS)
    out = jax.ShapeDtypeStruct((m, loads), F32)
    multipliers, residual = pl.pallas_call(
        functools.partial(kernel, shape),
        out_shape=(out, out),
        in_specs=[vmem, vmem, vmem, vmem, smem, vmem],
        out_specs=(vmem, vmem),
        scratch_shapes=[
            square, square, square, square, rows, rows, rows, rows,
            pltpu.VMEM((m, total), BF16),
            rows, rows, rows,
            pltpu.VMEM((2 * SUB, m), BF16),
            pltpu.VMEM((SUB, m), F32),
            pltpu.VMEM((ITERS + 1, SUB, LANES), F32),
            pltpu.VMEM((ITERS + 1, lines * nz, SUB, LANES), F32),
            pltpu.VMEM((lines, csize, cwide), F32),
            pltpu.VMEM((lines, line_rows + 2 * SUB, cwide), F32),
            pltpu.VMEM((lines * line_rows, cwide), F32),
            pltpu.VMEM((2 * total, lines * line_rows), BF16),
            dma((slots,)), dma((slots,)), dma((slots,)), dma((slots,)),
            dma((lines,)), dma((ITERS + 1, lines)), dma((lines,)), dma((lines,)),
        ],
        compiler_params=pltpu.CompilerParams(
            collective_id=0, has_side_effects=True, vmem_limit_bytes=48 * 1024 * 1024),
    )(dual_blocks[0, 0, 0], load_terms[0, 0, 0], row_order[0, 0], mode_rows[0, 0, 0].T,
      mode_count.reshape(1), coarse_inverse[0, 0])
    return multipliers[None, None, None], residual[None, None, None]


def solution(mesh):
    shape = tuple(mesh.shape[name] for name in ("gx", "gy", "gz"))
    in_specs = (
        P("gx", "gy", "gz", None, None),
        P("gx", "gy", "gz", None, None),
        P("gx", "gy", "gz", None),
        P("gx", "gy", "gz", None, None),
        P("gx", "gy", "gz"),
        P("gx", "gy", None, None),
    )
    out_specs = (P("gx", "gy", "gz", None, None), P("gx", "gy", "gz", None, None))
    return jax.shard_map(functools.partial(local, shape), mesh=mesh, in_specs=in_specs,
                         out_specs=out_specs, check_vma=False)
```

time: 305 us -> 53.4 us (0.18)
  starting transfers between devices: 127 us -> 0 us
  waiting for transfers between devices: 66 us -> 0 us
  local copies, waits for them, and re-layouts: 58.4 us -> 6.23 us
  Pallas kernels: 0 us -> 45.4 us
  blocking collectives: 24.2 us -> 0 us
  other arithmetic: 14.5 us -> 0 us
  matrix products: 8.02 us -> 0 us
    ppermute x42 -> x0, starting transfers between devices: 127 us -> none  [from_behind(): return lax.ppermute(block, axis, route)]
    ppermute x42 -> x0, waiting for transfers between devices: 66 us -> none  [from_behind(): return lax.ppermute(block, axis, route)]
    pallas_call x0 -> x1, Pallas kernels: none -> 45.4 us  [local(): pl.pallas_call(functools.partial(kernel, shape), out_shape=(out, out), in...]
    gather x6 -> x0, local copies, waits for them, and re-layouts: 28.4 us -> none  [the longest x1 7.9 us: local(): jnp.take(jnp.take(dual_blocks[0, 0, 0], packing, axis=0), packing, axis=1)]
    all_gather x4 -> x0, blocking collectives: 24.2 us -> none  [the longest x3 17.7 us: coarse_amplitude(): lax.all_gather(project, 'gz', axis=0, tiled=True)]
    unnamed x301 -> x12, local copies, waits for them, and re-layouts: 21.9 us -> 6.23 us
    dot_general x16 -> x0, matrix products: 8.02 us -> none  [the longest x3 3.04 us: apply_operator(): jnp.dot(dual_packed, rounded, preferred_element_type=jnp.float32)]
    sort x1 -> x0, other arithmetic: 5.05 us -> none  [local(): unpacking = jnp.argsort(packing)]
  transfers between devices with their start and end apart: 42 -> 0, of which waited for: 33 -> 0; matrix products, arithmetic and copies ran while one was open for 9% -> 0% of each run, Pallas kernels for 0% -> 0%
where the time goes in v1:
time: 53.4 us; the launch traced here: 52.9 us
  Pallas kernels  45.4 us (85%)
  local copies, waits for them, and re-layouts  6.23 us (12%)
  between operations  1.3 us (2%)
    pallas_call x1, Pallas kernels, local(): pl.pallas_call(functools.partial(kernel, shape), out_shape=(out, out), in...  45.4 us
    unnamed x12, local copies, waits for them, and re-layouts  6.23 us

profile of v1, /device:TPU:1, one launch (start us, length us, event | category | flops | bytes accessed | tf_op | source)
XLA Modules:
  0.0 52.9 jit_solution(15516282749460595520)
XLA Ops:
  1.3 0.0 copy-start
  1.3 1.6 %copy-done = bf16[1,1,1,1024,1024]{4,3,2,1,0:T(8,128)(2,1)S(1)} copy-done((bf16[1,1,1,1024,1024]{4,3,2,1,0:T(8,128)(2,1)S(1)}, bf16[1,1,1,1024,1024]{4,3,2,1,0:T(8,128)(2,1)}, u32[]{:S(2)}) %copy-start) | copy-done | bytes 2097176
  2.9 0.0 copy-start.1
  2.9 0.9 %copy-done.1 = bf16[1,1,1,1024,128]{4,3,2,1,0:T(8,128)(2,1)S(1)} copy-done((bf16[1,1,1,1024,128]{4,3,2,1,0:T(8,128)(2,1)S(1)}, bf16[1,1,1,1024,128]{4,3,2,1,0:T(8,128)(2,1)}, u32[]{:S(2)}) %copy-start.1) | copy-done | bytes 262168
  3.8 0.0 copy-start.2
  3.8 0.7 %copy-done.2 = bf16[1,1,1,1024,6]{3,4,2,1,0:T(8,128)(2,1)S(1)} copy-done((bf16[1,1,1,1024,6]{3,4,2,1,0:T(8,128)(2,1)S(1)}, bf16[1,1,1,1024,6]{3,4,2,1,0:T(8,128)(2,1)}, u32[]{:S(2)}) %copy-start.2) | copy-done | bytes 12312
  4.5 0.0 copy-start.3
  4.5 0.7 %copy-done.3 = f32[1,1,24,24]{3,2,1,0:T(8,128)S(1)} copy-done((f32[1,1,24,24]{3,2,1,0:T(8,128)S(1)}, f32[1,1,24,24]{3,2,1,0:T(8,128)}, u32[]{:S(2)}) %copy-start.3) | copy-done | bytes 2328
  5.2 0.0 copy-start.4
  5.2 0.7 %copy-done.4 = s32[1,1,1,1024]{3,2,1,0:T(1,128)S(1)} copy-done((s32[1,1,1,1024]{3,2,1,0:T(1,128)S(1)}, s32[1,1,1,1024]{3,2,1,0:T(1,128)}, u32[]{:S(2)}) %copy-start.4) | copy-done | bytes 4120
  5.9 45.4 %shard_map.77 = (f32[1024,128]{1,0:T(8,128)S(1)}, f32[1024,128]{1,0:T(8,128)S(1)}) custom-call(bf16[1024,1024]{1,0:T(8,128)(2,1)S(1)} %bitcast.11, bf16[1024,128]{1,0:T(8,128)(2,1)S(1)} %bitcast.14, s32[1,1024]{1,0:T(1,128)S(1)} %bitcast.17, bf16[6,1024]{1,0:T(8,128)(2,1)S(1)} %bitcast.15, s32[1]{0:T(128)} %bitcast.10.count_ref, f32[24,24]{1,0:T(8,128)S(1)} %bitcast.16), custom_call_target="tpu_custom_call" | custom-call | tf_op jit(solution)/shard_map/pallas_call | solution.py:361
  51.3 0.8 %copy.11 = f32[1,1,1,1024,128]{4,3,2,1,0:T(8,128)} copy(f32[1,1,1,1024,128]{4,3,2,1,0:T(8,128)S(1)} %bitcast.13) | data formatting | bytes 1048576
  52.1 0.8 %copy.12 = f32[1,1,1,1024,128]{4,3,2,1,0:T(8,128)} copy(f32[1,1,1,1024,128]{4,3,2,1,0:T(8,128)S(1)} %bitcast.12) | data formatting | bytes 1048576
Async XLA Ops:
  1.3 1.6 %copy-start = (bf16[1,1,1,1024,1024]{4,3,2,1,0:T(8,128)(2,1)S(1)}, bf16[1,1,1,1024,1024]{4,3,2,1,0:T(8,128)(2,1)}, u32[]{:S(2)}) copy-start(bf16[1,1,1,1024,1024]{4,3,2,1,0:T(8,128)(2,1)} %param.6) | copy-start | bytes 6291460
  2.9 0.9 %copy-start.1 = (bf16[1,1,1,1024,128]{4,3,2,1,0:T(8,128)(2,1)S(1)}, bf16[1,1,1,1024,128]{4,3,2,1,0:T(8,128)(2,1)}, u32[]{:S(2)}) copy-start(bf16[1,1,1,1024,128]{4,3,2,1,0:T(8,128)(2,1)} %param.7) | copy-start | bytes 786436
  3.8 0.7 %copy-start.2 = (bf16[1,1,1,1024,6]{3,4,2,1,0:T(8,128)(2,1)S(1)}, bf16[1,1,1,1024,6]{3,4,2,1,0:T(8,128)(2,1)}, u32[]{:S(2)}) copy-start(bf16[1,1,1,1024,6]{3,4,2,1,0:T(8,128)(2,1)} %param.9) | copy-start | bytes 36868
  4.5 0.7 %copy-start.3 = (f32[1,1,24,24]{3,2,1,0:T(8,128)S(1)}, f32[1,1,24,24]{3,2,1,0:T(8,128)}, u32[]{:S(2)}) copy-start(f32[1,1,24,24]{3,2,1,0:T(8,128)} %param.11) | copy-start | bytes 6916
  5.2 0.7 %copy-start.4 = (s32[1,1,1,1024]{3,2,1,0:T(1,128)S(1)}, s32[1,1,1,1024]{3,2,1,0:T(1,128)}, u32[]{:S(2)}) copy-start(s32[1,1,1,1024]{3,2,1,0:T(1,128)} %param.8) | copy-start | bytes 12292

commit v2 on v1

--- a/solution.py
+++ b/solution.py
@@ -16,10 +16,10 @@
 
 MESH = pl.DeviceIdType.MESH
 LANES = 128
+VMEM_BYTES = 62 * 1024 * 1024
 SUB = 8
 F32 = jnp.float32
 BF16 = jnp.bfloat16
-HIGHEST = lax.Precision.HIGHEST
 
 
 def slot_table():
@@ -60,8 +60,9 @@
     return jnp.concatenate([high, low], axis=1)
 
 
-def kernel(shape, dual_ref, load_ref, order_ref, modes_ref, count_ref, inverse_ref,
-           mult_out, res_out,
+def kernel(shape, dual_hbm, load_hbm, order_hbm, modes_hbm, count_ref, inverse_hbm,
+           mult_hbm, res_hbm,
+           mult_out, res_out, written, dual_ref, load_ref, order_ref, modes_ref, inverse_ref, fetched,
            perm, perm_t, half_packed, packed, image, received, own_modes, far_modes, wide,
            residual, direction, multipliers, modes_t, mode_pad,
            project_out, projects, inverses, select_pad, select_all, coarse,
@@ -73,6 +74,13 @@
     csize = inverse_ref.shape[0]
     cwide = inverses.shape[2]
     line_rows = nz * SUB
+    fetch = [pltpu.make_async_copy(source, target, fetched.at[k]) for k, (source, target) in enumerate(
+        ((order_hbm, order_ref), (load_hbm, load_ref), (modes_hbm, modes_ref),
+         (inverse_hbm, inverse_ref), (dual_hbm, dual_ref)))]
+    for copy in fetch:
+        copy.start()
+    results = [pltpu.make_async_copy(mult_out, mult_hbm, written.at[0]),
+               pltpu.make_async_copy(res_out, res_hbm, written.at[1])]
     barrier = pltpu.get_barrier_semaphore()
 
     def line_exists(line):
@@ -178,6 +186,7 @@
         both = jnp.dot(modes_t[...], halves(residual[...]), preferred_element_type=F32)
         return (both[:, :LANES] + both[:, LANES:])[:SUB]
 
+    fetch[0].wait()
     order_rows = jnp.broadcast_to(order_ref[...].astype(F32), (LANES, m))
     order_cols = order_rows.T
     lane = lax.broadcasted_iota(jnp.int32, (m, LANES), 1).astype(F32)
@@ -185,6 +194,8 @@
         hit = order_cols == lane + float(part * LANES)
         perm[:, part * LANES:(part + 1) * LANES] = jnp.where(hit, 1.0, 0.0).astype(BF16)
 
+    fetch[1].wait()
+    fetch[2].wait()
     mode_pad[...] = jnp.zeros_like(mode_pad)
     mode_pad[pl.ds(0, nmode)] = modes_ref[...].astype(F32)
     repeated = jnp.concatenate([mode_pad[...]] * (LANES // SUB), axis=0).T.astype(BF16)
@@ -193,6 +204,7 @@
     image[...] = both[:, :LANES]
     own_modes[...] = both[:, LANES:]
 
+    fetch[3].wait()
     inverses[OWN] = jnp.zeros((csize, cwide), F32)
     inverses[OWN, :, pl.ds(0, csize)] = inverse_ref[...]
     publish(0, jnp.full((SUB, LANES), count_ref[0], jnp.int32).astype(F32))
@@ -232,6 +244,8 @@
         perm_t[pl.ds(base, tile)] = jnp.where(row == order_row, 1.0, 0.0).astype(BF16)
         return carry
     lax.fori_loop(0, m // tile, transpose_tile, 0)
+
+    fetch[4].wait()
 
     def first_product(step, carry):
         base = pl.multiple_of(step * tile, tile)
@@ -272,17 +286,21 @@
                 inverse_copy(8 - index).wait_recv()
                 inverse_copy(index).wait_send()
     total = coarse.shape[0] // 2
-    lane_all = lax.broadcasted_iota(jnp.int32, (3 * SUB, len(LINES) * line_rows), 1)
-    strips = []
+    lefts = []
     for index in range(len(LINES)):
         near = select_pad[index, pl.ds(pl.multiple_of(iz * SUB, SUB), 3 * SUB)]
-        left = jnp.dot(near[:, :csize], inverses[index], precision=HIGHEST, preferred_element_type=F32)
-        strip = lax.dot_general(left, select_all[...], (((1,), (1,)), ((), ())),
-                                precision=HIGHEST, preferred_element_type=F32)
-        inside = (lane_all >= index * line_rows) & (lane_all < (index + 1) * line_rows)
-        strips.append(jnp.where(inside, strip, 0.0))
-    strips.append(jnp.zeros((total - BLOCKS * SUB, len(LINES) * line_rows), F32))
-    whole = jnp.concatenate(strips, axis=0)
+        both = jnp.dot(near[:, :csize].astype(BF16), halves(inverses[index]), preferred_element_type=F32)
+        lefts.append(both)
+    lefts.append(jnp.zeros((total - BLOCKS * SUB, 2 * cwide), F32))
+    lefts = jnp.concatenate(lefts, axis=0).astype(BF16)
+    whole = jnp.zeros((total, len(LINES) * line_rows), F32)
+    for part in range(2):
+        whole = whole + lax.dot_general(
+            lefts[:, part * cwide:(part + 1) * cwide], select_all[...].astype(BF16),
+            (((1,), (1,)), ((), ())), preferred_element_type=F32)
+    row_line = lax.broadcasted_iota(jnp.int32, whole.shape, 0) // (3 * SUB)
+    lane_line = lax.broadcasted_iota(jnp.int32, whole.shape, 1) // line_rows
+    whole = jnp.where(row_line == lane_line, whole, 0.0)
     high = whole.astype(BF16)
     coarse[pl.ds(0, total)] = high
     coarse[pl.ds(total, total)] = (whole - high.astype(F32)).astype(BF16)
@@ -328,6 +346,7 @@
         def _():
             pair = jnp.dot(perm_t[...], halves(multipliers[...]), preferred_element_type=F32)
             mult_out[...] = pair[:, :LANES] + pair[:, LANES:]
+            results[0].start()
 
         wait_slots(image, received, send_a, recv_a)
         residual[...] = residual[...] - image[...] - received[...]
@@ -341,6 +360,18 @@
 
     pair = jnp.dot(perm_t[...], halves(residual[...]), preferred_element_type=F32)
     res_out[...] = pair[:, :LANES] + pair[:, LANES:]
+    results[1].start()
+    results[0].wait()
+    results[1].wait()
+
+
+def write_out(mult_ref, res_ref, mult_hbm, res_hbm, written):
+    copies = [pltpu.make_async_copy(mult_ref, mult_hbm, written.at[0]),
+              pltpu.make_async_copy(res_ref, res_hbm, written.at[1])]
+    for copy in copies:
+        copy.start()
+    for copy in copies:
+        copy.wait()
 
 
 def local(shape, dual_blocks, load_terms, row_order, mode_rows, mode_count, coarse_inverse):
@@ -351,7 +382,7 @@
     lines = len(LINES)
     line_rows = nz * SUB
     total = -(-BLOCKS * SUB // LANES) * LANES
-    vmem = pl.BlockSpec(memory_space=pltpu.VMEM)
+    hbm = pl.BlockSpec(memory_space=pltpu.HBM)
     smem = pl.BlockSpec(memory_space=pltpu.SMEM)
     rows = pltpu.VMEM((m, loads), F32)
     square = pltpu.VMEM((m, m), BF16)
@@ -361,9 +392,11 @@
     multipliers, residual = pl.pallas_call(
         functools.partial(kernel, shape),
         out_shape=(out, out),
-        in_specs=[vmem, vmem, vmem, vmem, smem, vmem],
-        out_specs=(vmem, vmem),
+        in_specs=[hbm, hbm, hbm, hbm, smem, hbm],
+        out_specs=(hbm, hbm),
         scratch_shapes=[
+            rows, rows, dma((2,)), square, pltpu.VMEM((m, loads), BF16), pltpu.VMEM((1, m), jnp.int32),
+            pltpu.VMEM((mode_rows.shape[4], m), BF16), pltpu.VMEM((csize, csize), F32), dma((5,)),
             square, square, square, square, rows, rows, rows, rows,
             pltpu.VMEM((m, total), BF16),
             rows, rows, rows,
@@ -379,9 +412,17 @@
             dma((lines,)), dma((ITERS + 1, lines)), dma((lines,)), dma((lines,)),
         ],
         compiler_params=pltpu.CompilerParams(
-            collective_id=0, has_side_effects=True, vmem_limit_bytes=48 * 1024 * 1024),
+            collective_id=0, has_side_effects=True, vmem_limit_bytes=VMEM_BYTES),
     )(dual_blocks[0, 0, 0], load_terms[0, 0, 0], row_order[0, 0], mode_rows[0, 0, 0].T,
       mode_count.reshape(1), coarse_inverse[0, 0])
+    multipliers, residual = pl.pallas_call(
+        write_out,
+        out_shape=(out, out),
+        in_specs=[hbm, hbm],
+        out_specs=(hbm, hbm),
+        scratch_shapes=[dma((2,))],
+        compiler_params=pltpu.CompilerParams(vmem_limit_bytes=VMEM_BYTES),
+    )(multipliers, residual)
     return multipliers[None, None, None], residual[None, None, None]
 
 

time: 53.4 us -> 79.1 us (1.48)
  Pallas kernels: 45.4 us -> 77.5 us
  local copies, waits for them, and re-layouts: 6.23 us -> 0 us
    pallas_call x0 -> x1, Pallas kernels: none -> 32.9 us  [local(): pl.pallas_call(write_out, out_shape=(out, out), in_specs=[hbm, hbm], out_...]
    unnamed x12 -> x0, local copies, waits for them, and re-layouts: 6.23 us -> none
    pallas_call x1, Pallas kernels: 45.4 us -> 44.6 us  [local(): pl.pallas_call(functools.partial(kernel, shape), out_shape=(out, out), in...]
where the time goes in v2:
time: 79.1 us; the launch traced here: 78.8 us
  Pallas kernels  77.5 us (98%)
  between operations  1.29 us (2%)
    pallas_call x1, Pallas kernels, local(): pl.pallas_call(functools.partial(kernel, shape), out_shape=(out, out), in...  44.6 us
    pallas_call x1, Pallas kernels, local(): pl.pallas_call(write_out, out_shape=(out, out), in_specs=[hbm, hbm], out_...  32.9 us

profile of v2, /device:TPU:1, one launch (start us, length us, event | category | flops | bytes accessed | tf_op | source)
XLA Modules:
  0.0 78.8 jit_solution(4386914379799855749)
XLA Ops:
  1.3 44.6 %shard_map.77 = (f32[1024,128]{1,0:T(8,128)}, f32[1024,128]{1,0:T(8,128)}) custom-call(bf16[1024,1024]{1,0:T(8,128)(2,1)} %bitcast.11, bf16[1024,128]{1,0:T(8,128)(2,1)} %bitcast.12, s32[1,1024]{1,0:T(1,128)} %bitcast.15, bf16[6,1024]{1,0:T(8,128)(2,1)} %bitcast.13, s32[1]{0:T(128)} %bitcast.10.count_ref, f32[24,24]{1,0:T(8,128)} %bitcast.14), custom_call_target="tpu_custom_call" | custom-call | tf_op jit(solution)/shard_map/pallas_call | solution.py:392
  45.9 32.9 %shard_map.78 = (f32[1024,128]{1,0:T(8,128)}, f32[1024,128]{1,0:T(8,128)}) custom-call(f32[1024,128]{1,0:T(8,128)} %get-tuple-element.6.mult_ref, f32[1024,128]{1,0:T(8,128)} %get-tuple-element.7.res_ref), custom_call_target="tpu_custom_call" | custom-call | tf_op jit(solution)/shard_map/pallas_call | solution.py:418

commit v3 on v2

--- a/solution.py
+++ b/solution.py
@@ -365,12 +365,17 @@
     results[1].wait()
 
 
-def write_out(mult_ref, res_ref, mult_hbm, res_hbm, written):
-    copies = [pltpu.make_async_copy(mult_ref, mult_hbm, written.at[0]),
-              pltpu.make_async_copy(res_ref, res_hbm, written.at[1])]
-    for copy in copies:
+def write_out(mult_ref, res_ref, mult_hbm, res_hbm, mult_held, res_held, read, written):
+    inward = [pltpu.make_async_copy(mult_ref, mult_held, read.at[0]),
+              pltpu.make_async_copy(res_ref, res_held, read.at[1])]
+    outward = [pltpu.make_async_copy(mult_held, mult_hbm, written.at[0]),
+               pltpu.make_async_copy(res_held, res_hbm, written.at[1])]
+    for copy in inward:
         copy.start()
-    for copy in copies:
+    for first, second in zip(inward, outward):
+        first.wait()
+        second.start()
+    for copy in outward:
         copy.wait()
 
 
@@ -420,7 +425,7 @@
         out_shape=(out, out),
         in_specs=[hbm, hbm],
         out_specs=(hbm, hbm),
-        scratch_shapes=[dma((2,))],
+        scratch_shapes=[rows, rows, dma((2,)), dma((2,))],
         compiler_params=pltpu.CompilerParams(vmem_limit_bytes=VMEM_BYTES),
     )(multipliers, residual)
     return multipliers[None, None, None], residual[None, None, None]

time: 79.1 us -> 48.3 us (0.61)
  Pallas kernels: 77.5 us -> 46.6 us
    pallas_call x1, Pallas kernels: 32.9 us -> 2.04 us  [local(): pl.pallas_call(write_out, out_shape=(out, out), in_specs=[hbm, hbm], out_...]
where the time goes in v3:
time: 48.3 us; the launch traced here: 47.9 us
  Pallas kernels  46.6 us (96%)
  between operations  1.29 us (3%)
    pallas_call x1, Pallas kernels, local(): pl.pallas_call(functools.partial(kernel, shape), out_shape=(out, out), in...  44.6 us
    pallas_call x1, Pallas kernels, local(): pl.pallas_call(write_out, out_shape=(out, out), in_specs=[hbm, hbm], out_...  2.04 us

profile of v3, /device:TPU:1, one launch (start us, length us, event | category | flops | bytes accessed | tf_op | source)
XLA Modules:
  0.0 47.9 jit_solution(912103772416964193)
XLA Ops:
  1.3 44.6 %shard_map.77 = (f32[1024,128]{1,0:T(8,128)}, f32[1024,128]{1,0:T(8,128)}) custom-call(bf16[1024,1024]{1,0:T(8,128)(2,1)} %bitcast.11, bf16[1024,128]{1,0:T(8,128)(2,1)} %bitcast.12, s32[1,1024]{1,0:T(1,128)} %bitcast.15, bf16[6,1024]{1,0:T(8,128)(2,1)} %bitcast.13, s32[1]{0:T(128)} %bitcast.10.count_ref, f32[24,24]{1,0:T(8,128)} %bitcast.14), custom_call_target="tpu_custom_call" | custom-call | tf_op jit(solution)/shard_map/pallas_call | solution.py:397
  45.9 2.0 %shard_map.78 = (f32[1024,128]{1,0:T(8,128)}, f32[1024,128]{1,0:T(8,128)}) custom-call(f32[1024,128]{1,0:T(8,128)} %get-tuple-element.6.mult_ref, f32[1024,128]{1,0:T(8,128)} %get-tuple-element.7.res_ref), custom_call_target="tpu_custom_call" | custom-call | tf_op jit(solution)/shard_map/pallas_call | solution.py:423

commit v4 on v3

--- a/solution.py
+++ b/solution.py
@@ -64,11 +64,13 @@
            mult_hbm, res_hbm,
            mult_out, res_out, written, dual_ref, load_ref, order_ref, modes_ref, inverse_ref, fetched,
            perm, perm_t, half_packed, packed, image, received, own_modes, far_modes, wide,
+           wide_t, shares, arrived, line_project,
            residual, direction, multipliers, modes_t, mode_pad,
            project_out, projects, inverses, select_pad, select_all, coarse,
-           send_a, recv_a, send_m, recv_m, send_b, recv_b, send_i, recv_i):
+           send_a, recv_a, send_m, recv_m, send_c, recv_c, send_b, recv_b, send_i, recv_i):
     nx, ny, nz = shape
     ix, iy, iz = lax.axis_index("gx"), lax.axis_index("gy"), lax.axis_index("gz")
+    numbers = [(((o[0] + 1) * 3 + o[1] + 1) * 3 + o[2] + 1) for o, _, _ in SLOTS]
     m = dual_ref.shape[0]
     nmode = modes_ref.shape[0]
     csize = inverse_ref.shape[0]
@@ -178,6 +180,21 @@
             send_sem=send_i.at[index], recv_sem=recv_i.at[8 - index],
             device_id=(ix + line[0], iy + line[1], iz), device_id_type=MESH)
 
+    def share_copy(number):
+        offset = SLOTS[number][0]
+        other = [s[0] for s in SLOTS].index((-offset[0], -offset[1], -offset[2]))
+        return pltpu.make_async_remote_copy(
+            src_ref=shares.at[numbers[number]], dst_ref=arrived.at[other],
+            send_sem=send_c.at[number], recv_sem=recv_c.at[other],
+            device_id=(ix + offset[0], iy + offset[1], iz + offset[2]), device_id_type=MESH)
+
+    def share_arrival(number):
+        offset = SLOTS[number][0]
+        return pltpu.make_async_remote_copy(
+            src_ref=arrived.at[number], dst_ref=arrived.at[number],
+            send_sem=send_c.at[number], recv_sem=recv_c.at[number],
+            device_id=(ix + offset[0], iy + offset[1], iz + offset[2]), device_id_type=MESH)
+
     def publish(phase, block):
         project_out[phase] = block
         projects[phase, OWN * nz + iz] = block
@@ -214,7 +231,7 @@
     pl.semaphore_wait(barrier, lines_x * lines_y * nz - 1)
 
     every = range(len(SLOTS))
-    send_slots(image, received, send_a, recv_a, every)
+    send_slots(image, received.at[0], send_a, recv_a.at[0], every)
     send_blocks(0)
     for index, line in enumerate(LINES):
         if index != OWN:
@@ -223,10 +240,11 @@
                 inverse_copy(index).start()
     send_slots(own_modes, far_modes, send_m, recv_m, every)
 
-    for offset, begin, width in SLOTS:
+    for number, (offset, begin, width) in enumerate(SLOTS):
         @pl.when(jnp.logical_not(slot_exists(offset)))
-        def _(begin=begin, width=width):
-            received[pl.ds(begin, width)] = jnp.zeros((width, LANES), F32)
+        def _(number=number, begin=begin, width=width):
+            arrived[number] = jnp.zeros((SUB, LANES), F32)
+            received[:, pl.ds(begin, width)] = jnp.zeros((2, width, LANES), F32)
             far_modes[pl.ds(begin, width)] = jnp.zeros((width, LANES), F32)
     for index, line in enumerate(LINES):
         @pl.when(jnp.logical_not(line_exists(line)))
@@ -254,10 +272,11 @@
         return carry
     lax.fori_loop(0, m // tile, first_product, 0)
 
-    wait_slots(image, received, send_a, recv_a)
-    residual[...] = image[...] + received[...]
+    wait_slots(image, received.at[0], send_a, recv_a.at[0])
+    residual[...] = image[...] + received[0]
     wait_blocks(0)
-    publish(1, project())
+    line_project[...] = project()
+    publish(1, line_project[...])
     send_blocks(1)
 
     def second_product(step, carry):
@@ -306,7 +325,6 @@
     coarse[pl.ds(total, total)] = (whole - high.astype(F32)).astype(BF16)
 
     wait_slots(own_modes, far_modes, send_m, recv_m)
-    numbers = [(((o[0] + 1) * 3 + o[1] + 1) * 3 + o[2] + 1) for o, _, _ in SLOTS]
     row_block = jnp.concatenate(
         [jnp.full((SLOTS[k][2], LANES), numbers[k], jnp.int32) for k in every], axis=0)
     lane_row = lax.broadcasted_iota(jnp.int32, (m, LANES), 1)
@@ -315,10 +333,10 @@
         value = jnp.where(block == row_block, far_modes[...],
                           jnp.where(block == BLOCKS // 2, own_modes[...], 0.0))
         wide[:, part * LANES:(part + 1) * LANES] = value.astype(BF16)
+        wide_t[part * LANES:(part + 1) * LANES] = value.T.astype(BF16)
 
     direction[...] = jnp.zeros_like(direction)
     multipliers[...] = jnp.zeros_like(multipliers)
-    faces = 6 * FACE
     pairs = coefficients()
 
     def iteration(step, carry):
@@ -336,11 +354,33 @@
         direction[...] = now
         multipliers[...] = multipliers[...] + now
         rounded = now.astype(BF16)
-        image[pl.ds(0, faces)] = jnp.dot(packed[pl.ds(0, faces)], rounded, preferred_element_type=F32)
-        send_slots(image, received, send_a, recv_a, range(6))
-        image[pl.ds(faces, m - faces)] = jnp.dot(
-            packed[pl.ds(faces, m - faces)], rounded, preferred_element_type=F32)
-        send_slots(image, received, send_a, recv_a, range(6, len(SLOTS)))
+        image[...] = jnp.dot(packed[...], rounded, preferred_element_type=F32)
+        parity = lax.rem(step + 1, 2)
+
+        @pl.when(step < ITERS - 1)
+        def _():
+            both = jnp.dot(wide_t[...], halves(image[...]), preferred_element_type=F32)
+            shares[...] = (both[:, :LANES] + both[:, LANES:]).reshape(total // SUB, SUB, LANES)
+            for number in every:
+                @pl.when(slot_exists(SLOTS[number][0]))
+                def _(number=number):
+                    share_copy(number).start()
+        send_slots(image, received.at[parity], send_a, recv_a.at[parity], every)
+
+        @pl.when(step < ITERS - 1)
+        def _():
+            for number in every:
+                @pl.when(slot_exists(SLOTS[number][0]))
+                def _(number=number):
+                    share_arrival(number).wait_recv()
+                    share_copy(number).wait_send()
+            terms = [shares[BLOCKS // 2]] + [arrived[number] for number in every]
+            while len(terms) > 1:
+                terms = [terms[k] + terms[k + 1] if k + 1 < len(terms) else terms[k]
+                         for k in range(0, len(terms), 2)]
+            line_project[...] = line_project[...] - terms[0]
+            publish(step + 2, line_project[...])
+            send_blocks(step + 2)
 
         @pl.when(step == ITERS - 1)
         def _():
@@ -348,13 +388,8 @@
             mult_out[...] = pair[:, :LANES] + pair[:, LANES:]
             results[0].start()
 
-        wait_slots(image, received, send_a, recv_a)
-        residual[...] = residual[...] - image[...] - received[...]
-
-        @pl.when(step < ITERS - 1)
-        def _():
-            publish(step + 2, project())
-            send_blocks(step + 2)
+        wait_slots(image, received.at[parity], send_a, recv_a.at[parity])
+        residual[...] = residual[...] - image[...] - received[parity]
         return carry
     lax.fori_loop(0, ITERS, iteration, 0)
 
@@ -402,8 +437,12 @@
         scratch_shapes=[
             rows, rows, dma((2,)), square, pltpu.VMEM((m, loads), BF16), pltpu.VMEM((1, m), jnp.int32),
             pltpu.VMEM((mode_rows.shape[4], m), BF16), pltpu.VMEM((csize, csize), F32), dma((5,)),
-            square, square, square, square, rows, rows, rows, rows,
+            square, square, square, square, rows, pltpu.VMEM((2, m, loads), F32), rows, rows,
             pltpu.VMEM((m, total), BF16),
+            pltpu.VMEM((total, m), BF16),
+            pltpu.VMEM((total // SUB, SUB, LANES), F32),
+            pltpu.VMEM((slots, SUB, LANES), F32),
+            pltpu.VMEM((SUB, LANES), F32),
             rows, rows, rows,
             pltpu.VMEM((2 * SUB, m), BF16),
             pltpu.VMEM((SUB, m), F32),
@@ -413,7 +452,7 @@
             pltpu.VMEM((lines, line_rows + 2 * SUB, cwide), F32),
             pltpu.VMEM((lines * line_rows, cwide), F32),
             pltpu.VMEM((2 * total, lines * line_rows), BF16),
-            dma((slots,)), dma((slots,)), dma((slots,)), dma((slots,)),
+            dma((slots,)), dma((2, slots)), dma((slots,)), dma((slots,)), dma((slots,)), dma((slots,)),
             dma((lines,)), dma((ITERS + 1, lines)), dma((lines,)), dma((lines,)),
         ],
         compiler_params=pltpu.CompilerParams(

time: 48.3 us -> 47.4 us (0.981)
  Pallas kernels: 46.6 us -> 46 us
    pallas_call x1, Pallas kernels: 44.6 us -> 43.9 us  [local(): pl.pallas_call(functools.partial(kernel, shape), out_shape=(out, out), in...]
where the time goes in v4:
time: 47.4 us; the launch traced here: 47.2 us
  Pallas kernels  46 us (97%)
  between operations  1.29 us (3%)
    pallas_call x1, Pallas kernels, local(): pl.pallas_call(functools.partial(kernel, shape), out_shape=(out, out), in...  43.9 us
    pallas_call x1, Pallas kernels, local(): pl.pallas_call(write_out, out_shape=(out, out), in_specs=[hbm, hbm], out_...  2.04 us

profile of v4, /device:TPU:1, one launch (start us, length us, event | category | flops | bytes accessed | tf_op | source)
XLA Modules:
  0.0 47.2 jit_solution(14991003034725717507)
XLA Ops:
  1.3 43.9 %shard_map.77 = (f32[1024,128]{1,0:T(8,128)}, f32[1024,128]{1,0:T(8,128)}) custom-call(bf16[1024,1024]{1,0:T(8,128)(2,1)} %bitcast.11, bf16[1024,128]{1,0:T(8,128)(2,1)} %bitcast.12, s32[1,1024]{1,0:T(1,128)} %bitcast.15, bf16[6,1024]{1,0:T(8,128)(2,1)} %bitcast.13, s32[1]{0:T(128)} %bitcast.10.count_ref, f32[24,24]{1,0:T(8,128)} %bitcast.14), custom_call_target="tpu_custom_call" | custom-call | tf_op jit(solution)/shard_map/pallas_call | solution.py:432
  45.2 2.0 %shard_map.78 = (f32[1024,128]{1,0:T(8,128)}, f32[1024,128]{1,0:T(8,128)}) custom-call(f32[1024,128]{1,0:T(8,128)} %get-tuple-element.6.mult_ref, f32[1024,128]{1,0:T(8,128)} %get-tuple-element.7.res_ref), custom_call_target="tpu_custom_call" | custom-call | tf_op jit(solution)/shard_map/pallas_call | solution.py:462

commit v5 on v4

--- a/solution.py
+++ b/solution.py
@@ -17,6 +17,7 @@
 MESH = pl.DeviceIdType.MESH
 LANES = 128
 VMEM_BYTES = 62 * 1024 * 1024
+PIECES = 4
 SUB = 8
 F32 = jnp.float32
 BF16 = jnp.bfloat16
@@ -71,7 +72,6 @@
     nx, ny, nz = shape
     ix, iy, iz = lax.axis_index("gx"), lax.axis_index("gy"), lax.axis_index("gz")
     numbers = [(((o[0] + 1) * 3 + o[1] + 1) * 3 + o[2] + 1) for o, _, _ in SLOTS]
-    m = dual_ref.shape[0]
     nmode = modes_ref.shape[0]
     csize = inverse_ref.shape[0]
     cwide = inverses.shape[2]
@@ -81,8 +81,11 @@
          (inverse_hbm, inverse_ref), (dual_hbm, dual_ref)))]
     for copy in fetch:
         copy.start()
-    results = [pltpu.make_async_copy(mult_out, mult_hbm, written.at[0]),
-               pltpu.make_async_copy(res_out, res_hbm, written.at[1])]
+    m = dual_ref.shape[0]
+    cut = m // 2
+    results = [pltpu.make_async_copy(mult_out, mult_hbm, written.at[0])] + [
+        pltpu.make_async_copy(res_out.at[pl.ds(k * cut, cut)], res_hbm.at[pl.ds(k * cut, cut)], written.at[1 + k])
+        for k in range(2)]
     barrier = pltpu.get_barrier_semaphore()
 
     def line_exists(line):
@@ -238,7 +241,6 @@
             @pl.when(line_exists(line))
             def _(index=index):
                 inverse_copy(index).start()
-    send_slots(own_modes, far_modes, send_m, recv_m, every)
 
     for number, (offset, begin, width) in enumerate(SLOTS):
         @pl.when(jnp.logical_not(slot_exists(offset)))
@@ -271,6 +273,7 @@
             dual_ref[pl.ds(base, tile)], perm_t[...], preferred_element_type=F32).astype(BF16)
         return carry
     lax.fori_loop(0, m // tile, first_product, 0)
+    send_slots(own_modes, far_modes, send_m, recv_m, every)
 
     wait_slots(image, received.at[0], send_a, recv_a.at[0])
     residual[...] = image[...] + received[0]
@@ -393,18 +396,23 @@
         return carry
     lax.fori_loop(0, ITERS, iteration, 0)
 
-    pair = jnp.dot(perm_t[...], halves(residual[...]), preferred_element_type=F32)
-    res_out[...] = pair[:, :LANES] + pair[:, LANES:]
-    results[1].start()
-    results[0].wait()
-    results[1].wait()
+    parts = halves(residual[...])
+    for k in range(2):
+        pair = jnp.dot(perm_t[pl.ds(k * cut, cut)], parts, preferred_element_type=F32)
+        res_out[pl.ds(k * cut, cut)] = pair[:, :LANES] + pair[:, LANES:]
+        results[1 + k].start()
+    for copy in results:
+        copy.wait()
 
 
 def write_out(mult_ref, res_ref, mult_hbm, res_hbm, mult_held, res_held, read, written):
-    inward = [pltpu.make_async_copy(mult_ref, mult_held, read.at[0]),
-              pltpu.make_async_copy(res_ref, res_held, read.at[1])]
-    outward = [pltpu.make_async_copy(mult_held, mult_hbm, written.at[0]),
-               pltpu.make_async_copy(res_held, res_hbm, written.at[1])]
+    rows = mult_ref.shape[0] // PIECES
+    inward, outward = [], []
+    for piece in range(PIECES):
+        span = pl.ds(piece * rows, rows)
+        for k, (source, held, target) in enumerate(((mult_ref, mult_held, mult_hbm), (res_ref, res_held, res_hbm))):
+            inward.append(pltpu.make_async_copy(source.at[span], held.at[span], read.at[k, piece]))
+            outward.append(pltpu.make_async_copy(held.at[span], target.at[span], written.at[k, piece]))
     for copy in inward:
         copy.start()
     for first, second in zip(inward, outward):
@@ -435,7 +443,7 @@
         in_specs=[hbm, hbm, hbm, hbm, smem, hbm],
         out_specs=(hbm, hbm),
         scratch_shapes=[
-            rows, rows, dma((2,)), square, pltpu.VMEM((m, loads), BF16), pltpu.VMEM((1, m), jnp.int32),
+            rows, rows, dma((3,)), square, pltpu.VMEM((m, loads), BF16), pltpu.VMEM((1, m), jnp.int32),
             pltpu.VMEM((mode_rows.shape[4], m), BF16), pltpu.VMEM((csize, csize), F32), dma((5,)),
             square, square, square, square, rows, pltpu.VMEM((2, m, loads), F32), rows, rows,
             pltpu.VMEM((m, total), BF16),
@@ -464,7 +472,7 @@
         out_shape=(out, out),
         in_specs=[hbm, hbm],
         out_specs=(hbm, hbm),
-        scratch_shapes=[rows, rows, dma((2,)), dma((2,))],
+        scratch_shapes=[rows, rows, dma((2, PIECES)), dma((2, PIECES))],
         compiler_params=pltpu.CompilerParams(vmem_limit_bytes=VMEM_BYTES),
     )(multipliers, residual)
     return multipliers[None, None, None], residual[None, None, None]

time: 47.4 us -> 47.2 us (level)
  no operation moved by 1% of the time
where the time goes in v5:
time: 47.2 us; the launch traced here: 47 us
  Pallas kernels  45.7 us (97%)
  between operations  1.29 us (3%)
    pallas_call x1, Pallas kernels, local(): pl.pallas_call(functools.partial(kernel, shape), out_shape=(out, out), in...  43.6 us
    pallas_call x1, Pallas kernels, local(): pl.pallas_call(write_out, out_shape=(out, out), in_specs=[hbm, hbm], out_...  2.09 us

profile of v5, /device:TPU:1, one launch (start us, length us, event | category | flops | bytes accessed | tf_op | source)
XLA Modules:
  0.0 47.0 jit_solution(17630712596102411764)
XLA Ops:
  1.3 43.6 %shard_map.77 = (f32[1024,128]{1,0:T(8,128)}, f32[1024,128]{1,0:T(8,128)}) custom-call(bf16[1024,1024]{1,0:T(8,128)(2,1)} %bitcast.11, bf16[1024,128]{1,0:T(8,128)(2,1)} %bitcast.12, s32[1,1024]{1,0:T(1,128)} %bitcast.15, bf16[6,1024]{1,0:T(8,128)(2,1)} %bitcast.13, s32[1]{0:T(128)} %bitcast.10.count_ref, f32[24,24]{1,0:T(8,128)} %bitcast.14), custom_call_target="tpu_custom_call" | custom-call | tf_op jit(solution)/shard_map/pallas_call | solution.py:440
  44.9 2.1 %shard_map.78 = (f32[1024,128]{1,0:T(8,128)}, f32[1024,128]{1,0:T(8,128)}) custom-call(f32[1024,128]{1,0:T(8,128)} %get-tuple-element.6.mult_ref, f32[1024,128]{1,0:T(8,128)} %get-tuple-element.7.res_ref), custom_call_target="tpu_custom_call" | custom-call | tf_op jit(solution)/shard_map/pallas_call | solution.py:470
